TPU v7x, 32 devices: a whole 2x2x4 slice. The times are simulated.
32 devices in a mesh: head: 4 (over y, x), blk: 8 (over z, core).
Axes of the slice: x: 2, y: 2, z: 4, core: 2. Of those that a mesh axis runs over, the one named last changes fastest.
Arguments:
- hidden_in: bfloat16 [3072, 1408], P('blk'), may hold values from -25 to 25
- queries: bfloat16 [3072, 1408], P('blk', 'head'), may hold values from -7.182936 to 7.182936
- keys: bfloat16 [3072, 1408], P('blk', 'head'), may hold values from -7.182936 to 7.182936
- values: bfloat16 [3072, 1408], P('blk', 'head'), may hold values from -10 to 10
- out_weight: bfloat16 [1408, 1408], P('head'), may hold values from -0.15625 to 0.15625
- out_bias: float32 [1408], replicated, may hold values from -3 to 3
- norm_gain: float32 [1408], replicated, may hold values from 0.1 to 1.9
- norm_bias: float32 [1408], replicated, may hold values from -3 to 3
- up_weight: bfloat16 [1408, 6144], P(None, 'head'), may hold values from -0.15625 to 0.15625
- up_bias: float32 [6144], P('head'), may hold values from -3 to 3
- down_weight: bfloat16 [6144, 1408], P('head'), may hold values from -0.078125 to 0.078125
- down_bias: float32 [1408], replicated, may hold values from -3 to 3
- merge_weight: bfloat16 [5632, 4096], P(None, 'head'), may hold values from -0.078125 to 0.078125
- merge_bias: float32 [4096], P('head'), may hold values from -3 to 3
- group_segments: int32 [768], P('blk'), may hold values from 0 to 15, never falling along the last dimension, each value on 1 to 576 neighbouring positions
- owner_slots: int32 [16], replicated, may hold values from 0 to 15, each once
Outputs:
- merged_out: bfloat16 [768, 4096], P('blk', 'head')
- state_rms: float32 [16], P('blk')
- logit_max: float32 [16, 16], P('blk', 'head')
Inputs may be any that keep to these rules, and one draw needn't show every extreme that they name: `group_segments`: request numbers never fall along the groups; every request number is used, each by 1 to 576 groups, and one request has exactly 576 groups. `owner_slots`: each slot number appears once.
All inputs are finite; a program needn't handle non-finite values.
Results may differ from a plain program's by a relative error of at most 0.013.
Values may be sent and summed in bfloat16 or wider, within the bound.
A program may use at most 128 MiB of HBM per device.

v0:
```python
import math

import jax
import jax.numpy as jnp
from jax import lax
from jax.sharding import PartitionSpec as P

HD = 88


NEGATIVE = -1e30
EPSILON = 1e-06


def body(
    hidden_in,
    queries,
    keys,
    values,
    out_weight,
    out_bias,
    norm_gain,
    norm_bias,
    up_weight,
    up_bias,
    down_weight,
    down_bias,
    merge_weight,
    merge_bias,
    group_segments,
    owner_slots,
):
    row_count = queries.shape[0]
    feat_width = queries.shape[1]
    head_count = feat_width // HD
    model_width = hidden_in.shape[1]
    score_scale = HD ** (-0.5)
    row_segments = jnp.repeat(group_segments, 4)
    segment_wire = row_segments.astype(jnp.bfloat16)
    segment_float = row_segments.astype(jnp.float32)
    query_heads = queries.reshape(row_count, head_count, HD)
    initial = (
        jnp.full((head_count, row_count), NEGATIVE, jnp.float32),
        jnp.zeros((head_count, row_count), jnp.float32),
        jnp.zeros((head_count, row_count, HD), jnp.float32),
    )
    key_piece = lax.all_gather(keys, "blk", axis=0, tiled=True)
    value_piece = lax.all_gather(values, "blk", axis=0, tiled=True)
    segment_piece = lax.all_gather(segment_wire, "blk", axis=0, tiled=True)
    piece_rows = key_piece.shape[0]
    key_block = math.gcd(piece_rows, 2048)

    def one_block(turn_index, carried):
        offset = turn_index * key_block
        block_keys = lax.dynamic_slice_in_dim(key_piece, offset, key_block, 0).reshape(
            key_block, head_count, HD
        )
        block_values = lax.dynamic_slice_in_dim(value_piece, offset, key_block, 0).reshape(
            key_block, head_count, HD
        )
        block_segments = lax.dynamic_slice_in_dim(segment_piece, offset, key_block, 0).astype(
            jnp.float32
        )
        old_max, old_sum, old_out = carried
        scores = (
            jnp.einsum("qhd,khd->hqk", query_heads, block_keys, preferred_element_type=jnp.float32)
            * score_scale
        )
        allowed = (segment_float[:, None] == block_segments[None, :])[None]
        scores = jnp.where(allowed, scores, NEGATIVE)
        new_max = jnp.maximum(old_max, jnp.max(scores, axis=-1))
        exponents = jnp.where(allowed, jnp.exp(scores - new_max[..., None]), 0.0)
        factor = jnp.exp(old_max - new_max)
        weights = exponents.astype(jnp.bfloat16)
        product = jnp.einsum(
            "hqk,khd->hqd", weights, block_values, preferred_element_type=jnp.float32
        )
        return (
            new_max,
            old_sum * factor + jnp.sum(exponents, axis=-1),
            old_out * factor[..., None] + product,
        )

    row_max, row_sum, row_out = lax.fori_loop(0, piece_rows // key_block, one_block, initial)
    attended = (
        jnp.transpose(row_out / row_sum[..., None], (1, 0, 2))
        .reshape(row_count, feat_width)
        .astype(jnp.bfloat16)
    )
    attention_part = jnp.dot(attended, out_weight, preferred_element_type=jnp.float32)
    mixed = (
        hidden_in.astype(jnp.float32)
        + lax.psum(attention_part.astype(jnp.bfloat16), "head").astype(jnp.float32)
        + out_bias
    )
    row_mean = jnp.mean(mixed, axis=-1, keepdims=True)
    centered = mixed - row_mean
    row_var = jnp.mean(centered * centered, axis=-1, keepdims=True)
    normed = (centered * lax.rsqrt(row_var + EPSILON) * norm_gain + norm_bias).astype(jnp.bfloat16)
    up_proj = jnp.dot(normed, up_weight, preferred_element_type=jnp.float32) + up_bias
    hidden_units = jax.nn.gelu(up_proj, approximate=False).astype(jnp.bfloat16)
    down_part = jnp.dot(hidden_units, down_weight, preferred_element_type=jnp.float32)
    state = mixed + lax.psum(down_part.astype(jnp.bfloat16), "head").astype(jnp.float32) + down_bias
    state_bf = state.astype(jnp.bfloat16)
    merged_rows = state_bf.reshape(row_count // 4, 4 * model_width)
    merged_out = (
        jnp.dot(merged_rows, merge_weight, preferred_element_type=jnp.float32) + merge_bias
    ).astype(jnp.bfloat16)
    request_total = owner_slots.shape[0]
    per_owner = request_total // lax.axis_size("blk")
    member = row_segments[None, :] == jnp.arange(request_total, dtype=jnp.int32)[:, None]
    squares = jnp.sum(state * state, axis=-1)
    request_sums = jnp.sum(jnp.where(member, squares[None, :], 0.0), axis=-1)
    counts = jnp.sum(member.astype(jnp.float32), axis=-1)
    request_max = jnp.max(jnp.where(member[None], row_max[:, None, :], NEGATIVE), axis=-1)
    slot_ids = lax.axis_index("blk") * per_owner + jnp.arange(per_owner, dtype=jnp.int32)
    mine = owner_slots[None, :] == slot_ids[:, None]
    ordering = owner_slots[None, :] == jnp.arange(request_total, dtype=jnp.int32)[:, None]
    ordered_sums = jnp.sum(jnp.where(ordering, request_sums[None, :], 0.0), axis=-1)
    ordered_counts = jnp.sum(jnp.where(ordering, counts[None, :], 0.0), axis=-1)
    own_sums, own_counts = (
        lax.psum_scatter(ordered_sums, "blk", scatter_dimension=0, tiled=True),
        lax.psum_scatter(ordered_counts, "blk", scatter_dimension=0, tiled=True),
    )
    global_request_max = lax.pmax(request_max, "blk")
    state_rms = jnp.sqrt(own_sums / (own_counts * model_width) + EPSILON)
    logit_max = jnp.transpose(
        jnp.max(jnp.where(mine[None], global_request_max[:, None, :], NEGATIVE), axis=-1)
    )
    return (merged_out, state_rms, logit_max)


def solution(mesh):
    in_specs = (
        P("blk", None),
        P("blk", "head"),
        P("blk", "head"),
        P("blk", "head"),
        P("head", None),
        P(),
        P(),
        P(),
        P(None, "head"),
        P("head"),
        P("head", None),
        P(),
        P(None, "head"),
        P("head"),
        P("blk"),
        P(),
    )
    out_specs = (P("blk", "head"), P("blk"), P("blk", "head"))
    return jax.shard_map(body, mesh=mesh, in_specs=in_specs, out_specs=out_specs, check_vma=False)
```

profile of v0, /device:TPU:0, one launch (start us, length us, event | category | flops | bytes accessed | tf_op | source)
XLA Modules:
  0.0 270.8 jit_solution(5214808285798442490)
XLA Ops:
  7.2 0.0 copy-start
  7.2 0.0 all-gather.4.cloned.1.call-start
  7.2 0.7 all-gather.4.cloned.1.call-update
  7.9 0.0 all-gather.6.cloned.1.call-start
  8.0 0.7 all-gather.6.cloned.1.call-update
  8.7 0.0 all-reduce.6.cloned.1.call-start
  8.7 0.7 broadcast_in_dim.157
  9.5 0.1 reshape.139
  9.6 14.4 %all-gather = bf16[8,1,384]{2,1,0:T(2,128)(2,1)S(1)} all-gather(bf16[1,1,384]{2,1,0:T(2,128)(2,1)S(1)} %reshape.142), channel_id=1, replica_groups=mesh['head'=4,'blk'=8] {'blk'}, dimensions={0}, use_global_device_ids=true | all-gather | bytes 6912 | tf_op jit(solution)/shard_map/all_gather | solution.py:49
  24.0 18.0 %all-gather.4.cloned.1.call-done = bf16[3072,352]{0,1:T(8,128)(2,1)} async-done(((bf16[384,352]{0,1:T(8,128)(2,1)}), bf16[3072,352]{0,1:T(8,128)(2,1)}) %all-gather.4.cloned.1.call-update) | async-done | bytes 2162704 | tf_op jit(solution)/shard_map/all_gather | solution.py:47
  42.0 30.8 %all-gather.6.cloned.1.call-done = bf16[3072,352]{0,1:T(8,128)(2,1)} async-done(((bf16[384,352]{0,1:T(8,128)(2,1)}), bf16[3072,352]{0,1:T(8,128)(2,1)}) %all-gather.6.cloned.1.call-update) | async-done | bytes 2162704 | tf_op jit(solution)/shard_map/all_gather | solution.py:48
  72.8 39.8 %while.18 = (s32[]{:T(128)}, f32[4,384]{1,0:T(4,128)S(1)}, f32[4,384]{1,0:T(4,128)S(1)}, f32[4,384,88]{1,2,0:T(8,128)S(1)}, bf16[3072]{0:T(1024)(128)(2,1)S(1)},...) while((s32[]{:T(128)}, f32[4,384]{1,0:T(4,128)S(1)}, ...), condition=%wide.region_3.4_spmd.clone, body=%wide.region_0.3_spmd.clone.sunk | while | flops 574903168 | bytes 52489844 | solution.py:84
  72.8 0.8 broadcast_in_dim.224
  73.6 0.1 reshape.154
  73.7 0.3 broadcast_compare_fusion.3
  74.0 1.4 constant_dynamic-slice_fusion.3
  75.5 4.0 %fusion.121 = (f32[4,384]{1,0:T(4,128)S(1)}, f32[4,1024,384]{2,1,0:T(8,128)}) fusion(pred[384,1024]{0,1:T(8,128)(4,1)S(1)} %broadcast_compare_fusion.3, bf16[1024,4,88]{0,2,1:T(8,128)(2,1)S(1)} %bitcast.46, bf16[384,4,88]{0,2,1:T(8,128)(2,1)S(1)} %copy-done.4), kind=kOutput, calls=%fused_computation.3.clone.1 | convolution fusion | flops 281541120 | bytes 7682048 | tf_op jit(solution)/shard_map/while/body/eval_jaxpr/qhd,khd->hqk/dot_general | solution.py:66
  79.4 4.5 %fusion.122 = f32[4,384]{1,0:T(4,128)S(1)} fusion(f32[4,1024,384]{2,1,0:T(8,128)} %get-tuple-element.290, f32[4,384]{1,0:T(4,128)S(1)} %select_maximum_fusion.2, pred[384,1024]{0,1:T(8,128)(4,1)S(1)} %broadcast_compare_fusion.3), kind=kLoop, calls=%fused_computation.5.clone.1 | loop fusion | flops 7862784 | bytes 6696960 | tf_op jit(solution)/shard_map/while/body/eval_jaxpr/reduce_sum | solution.py:80
  84.0 0.1 copy-done.1
  84.0 2.0 fusion.124
  86.1 0.0 copy-start.4
  86.1 0.8 broadcast_in_dim.224
  86.9 0.1 reshape.154
  87.0 0.3 broadcast_compare_fusion.3
  87.3 1.4 constant_dynamic-slice_fusion.3
  88.7 4.0 %fusion.121 = (f32[4,384]{1,0:T(4,128)S(1)}, f32[4,1024,384]{2,1,0:T(8,128)}) fusion(pred[384,1024]{0,1:T(8,128)(4,1)S(1)} %broadcast_compare_fusion.3, bf16[1024,4,88]{0,2,1:T(8,128)(2,1)S(1)} %bitcast.46, bf16[384,4,88]{0,2,1:T(8,128)(2,1)S(1)} %copy-done.4), kind=kOutput, calls=%fused_computation.3.clone.1 | convolution fusion | flops 281541120 | bytes 7682048 | tf_op jit(solution)/shard_map/while/body/eval_jaxpr/qhd,khd->hqk/dot_general | solution.py:66
  92.7 4.5 %fusion.122 = f32[4,384]{1,0:T(4,128)S(1)} fusion(f32[4,1024,384]{2,1,0:T(8,128)} %get-tuple-element.290, f32[4,384]{1,0:T(4,128)S(1)} %select_maximum_fusion.2, pred[384,1024]{0,1:T(8,128)(4,1)S(1)} %broadcast_compare_fusion.3), kind=kLoop, calls=%fused_computation.5.clone.1 | loop fusion | flops 7862784 | bytes 6696960 | tf_op jit(solution)/shard_map/while/body/eval_jaxpr/reduce_sum | solution.py:80
  97.2 0.1 copy-done.1
  97.3 2.0 fusion.124
  99.3 0.0 copy-start.4
  99.4 0.8 broadcast_in_dim.224
  100.1 0.1 reshape.154
  100.3 0.3 broadcast_compare_fusion.3
  100.5 1.4 constant_dynamic-slice_fusion.3
  102.0 4.0 %fusion.121 = (f32[4,384]{1,0:T(4,128)S(1)}, f32[4,1024,384]{2,1,0:T(8,128)}) fusion(pred[384,1024]{0,1:T(8,128)(4,1)S(1)} %broadcast_compare_fusion.3, bf16[1024,4,88]{0,2,1:T(8,128)(2,1)S(1)} %bitcast.46, bf16[384,4,88]{0,2,1:T(8,128)(2,1)S(1)} %copy-done.4), kind=kOutput, calls=%fused_computation.3.clone.1 | convolution fusion | flops 281541120 | bytes 7682048 | tf_op jit(solution)/shard_map/while/body/eval_jaxpr/qhd,khd->hqk/dot_general | solution.py:66
  106.0 4.5 %fusion.122 = f32[4,384]{1,0:T(4,128)S(1)} fusion(f32[4,1024,384]{2,1,0:T(8,128)} %get-tuple-element.290, f32[4,384]{1,0:T(4,128)S(1)} %select_maximum_fusion.2, pred[384,1024]{0,1:T(8,128)(4,1)S(1)} %broadcast_compare_fusion.3), kind=kLoop, calls=%fused_computation.5.clone.1 | loop fusion | flops 7862784 | bytes 6696960 | tf_op jit(solution)/shard_map/while/body/eval_jaxpr/reduce_sum | solution.py:80
  110.5 0.1 copy-done.1
  110.6 2.0 fusion.124
  112.6 0.0 copy-start.5
  112.7 1.8 convolution_convert_fusion.1
  114.5 0.0 all-reduce.6.cloned.1.call-update
  114.5 0.0 copy-start.10
  114.5 0.0 copy-start.11
  114.6 0.2 all-reduce.8.cloned.1.call-start
  114.8 52.5 %all-reduce.6.cloned.1.call-done = bf16[384,1408]{1,0:T(8,128)(2,1)} async-done(((bf16[384,1408]{1,0:T(8,128)(2,1)}), bf16[384,1408]{1,0:T(8,128)(2,1)}) %all-reduce.6.cloned.1.call-update) | async-done | bytes 1081360 | tf_op jit(solution)/shard_map/psum | solution.py:93
  167.3 1.8 fusion.25
  169.1 0.6 multiply_reduce_fusion.1
  169.7 0.0 copy-start.12
  169.7 0.0 copy-start.6
  169.7 12.3 %convolution_convert_fusion = bf16[384,1408]{1,0:T(8,128)(2,1)} fusion(bf16[1536,1408]{1,0:T(8,128)(2,1)} %param.28, bf16[1408,1536]{1,0:T(8,128)(2,1)} %param.26, f32[1536]{0:T(1024)S(1)} %copy-done.9, bf16[384,1408]{1,0:T(8,128)(2,1)S(1)} %copy-done.3, bf16[384,1408]{1,0:T(8,128)(2,1)S(1)} %copy-done.2, f32[1408]{0:T(1024)S(1)} %copy-done.10, ...), kind=kOutput, calls=%fused_computation.23 | convolution fusion | flops 3366223872 | bytes 11920896 | tf_op jit(solution)/shard_map/dot_general | solution.py:102
  182.0 0.0 all-reduce.8.cloned.1.call-update
  182.1 0.6 dynamic-slice
  183.3 0.1 broadcast_compare_fusion.1
  183.4 0.1 select_reduce_fusion
  183.5 16.3 %pmax.7 = f32[4,16]{1,0:T(4,128)S(1)} all-reduce(f32[4,16]{1,0:T(4,128)S(1)} %select_reduce_fusion), channel_id=1, replica_groups=mesh['head'=4,'blk'=8] {'blk'}, use_global_device_ids=true, to_apply=%region_16.17 | all-reduce | flops 64 | bytes 512 | tf_op jit(solution)/shard_map/pmax | solution.py:125
  199.8 0.7 select_reduce_fusion.4
  200.5 34.8 %all-reduce.8.cloned.1.call-done = bf16[384,1408]{1,0:T(8,128)(2,1)} async-done(((bf16[384,1408]{1,0:T(8,128)(2,1)}), bf16[384,1408]{1,0:T(8,128)(2,1)}) %all-reduce.8.cloned.1.call-update) | async-done | bytes 1081360 | tf_op jit(solution)/shard_map/psum | solution.py:103
  235.3 3.0 %multiply_reduce_fusion = (f32[384]{0:T(512)S(1)}, bf16[384,1408]{1,0:T(8,128)(2,1)}) fusion(bf16[384,1408]{1,0:T(8,128)(2,1)} %all-reduce.8.cloned.1.call-done, bf16[384,1408]{1,0:T(8,128)(2,1)S(1)} %copy-done.3, bf16[384,1408]{1,0:T(8,128)(2,1)S(1)} %copy-done.2, f32[1408]{0:T(1024)S(1)} %copy-done.6, f32[1408]{0:T(1024)S(1)} %copy-done.5), kind=kLoop, calls=%fused_computation.43 | loop fusion | flops 5406336 | bytes 4338176 | tf_op jit(solution)/shard_map/reduce_sum | solution.py:112
  238.4 0.1 select_reduce_fusion.1
  238.5 1.8 reshape.141
  240.3 0.1 select_reduce_fusion.3
  240.4 16.3 %all-reduce.2 = (f32[16]{0:T(128)S(1)}, f32[16]{0:T(128)S(1)}) all-reduce(f32[16]{0:T(128)S(1)} %get-tuple-element.198, f32[16]{0:T(128)S(1)} %get-tuple-element.197), channel_id=3, replica_groups=mesh['head'=4,'blk'=8] {'blk'}, use_global_device_ids=true, to_apply=%region_14.15.clone | all-reduce | flops 32 | bytes 256
  256.7 0.6 add_sqrt_fusion
  257.4 6.9 %fusion.57 = bf16[96,1024]{1,0:T(8,128)(2,1)} fusion(bf16[96,5632]{1,0:T(8,128)(2,1)S(1)} %reshape.141, bf16[5632,1024]{1,0:T(8,128)(2,1)} %param.30, f32[1024]{0:T(1024)S(1)} %copy-done.7), kind=kOutput, calls=%fused_computation.81 | convolution fusion | flops 1107492864 | bytes 12816384 | tf_op jit(solution)/shard_map/dot_general | solution.py:107
  (50 shorter events, 0.3 us)
Async XLA Ops:
  7.2 105.5 %copy-start = (bf16[352,1408]{1,0:T(8,128)(2,1)S(1)}, bf16[352,1408]{1,0:T(8,128)(2,1)}, u32[]{:S(2)}) copy-start(bf16[352,1408]{1,0:T(8,128)(2,1)} %param.22) | copy-start | bytes 2973700
  7.2 34.8 %all-gather.4.cloned.1.call-start = ((), (), s32[]{:S(2)}) async-start(), calls=%async_computation | async-start | bytes 2433024 | tf_op jit(solution)/shard_map/all_gather | solution.py:47
  7.9 64.9 %all-gather.6.cloned.1.call-start = ((), (), s32[]{:S(2)}) async-start(), calls=%async_computation.1 | async-start | bytes 2433024 | tf_op jit(solution)/shard_map/all_gather | solution.py:48
  8.7 158.6 %all-reduce.6.cloned.1.call-start = ((), (), s32[]{:S(2)}) async-start(), calls=%async_computation.2 | async-start | bytes 2162688 | tf_op jit(solution)/shard_map/psum | solution.py:93
  72.8 2.6 copy-start.4
  79.4 4.6 %copy-start.1 = (f32[4,1024,384]{2,1,0:T(8,128)S(1)}, f32[4,1024,384]{2,1,0:T(8,128)}, u32[]{:S(2)}) copy-start(f32[4,1024,384]{2,1,0:T(8,128)} %get-tuple-element.290) | copy-start | bytes 18874372 | tf_op jit(solution)/shard_map/while
  86.1 2.7 copy-start.4
  92.7 4.6 %copy-start.1 = (f32[4,1024,384]{2,1,0:T(8,128)S(1)}, f32[4,1024,384]{2,1,0:T(8,128)}, u32[]{:S(2)}) copy-start(f32[4,1024,384]{2,1,0:T(8,128)} %get-tuple-element.290) | copy-start | bytes 18874372 | tf_op jit(solution)/shard_map/while
  99.3 2.7 copy-start.4
  106.0 4.6 %copy-start.1 = (f32[4,1024,384]{2,1,0:T(8,128)S(1)}, f32[4,1024,384]{2,1,0:T(8,128)}, u32[]{:S(2)}) copy-start(f32[4,1024,384]{2,1,0:T(8,128)} %get-tuple-element.290) | copy-start | bytes 18874372 | tf_op jit(solution)/shard_map/while
  112.6 54.7 %copy-start.2 = (bf16[384,1408]{1,0:T(8,128)(2,1)S(1)}, bf16[384,1408]{1,0:T(8,128)(2,1)}, u32[]{:S(2)}) copy-start(bf16[384,1408]{1,0:T(8,128)(2,1)} %param.18) | copy-start | bytes 3244036
  112.6 54.7 %copy-start.5 = (f32[1408]{0:T(1024)S(1)}, f32[1408]{0:T(1024)}, u32[]{:S(2)}) copy-start(f32[1408]{0:T(1024)} %param.23) | copy-start | bytes 16900
  114.5 55.1 %copy-start.9 = (f32[1536]{0:T(1024)S(1)}, f32[1536]{0:T(1024)}, u32[]{:S(2)}) copy-start(f32[1536]{0:T(1024)} %param.27) | copy-start | bytes 18436
  114.5 55.1 %copy-start.10 = (f32[1408]{0:T(1024)S(1)}, f32[1408]{0:T(1024)}, u32[]{:S(2)}) copy-start(f32[1408]{0:T(1024)} %param.25) | copy-start | bytes 16900
  114.5 55.1 %copy-start.11 = (f32[1408]{0:T(1024)S(1)}, f32[1408]{0:T(1024)}, u32[]{:S(2)}) copy-start(f32[1408]{0:T(1024)} %param.24) | copy-start | bytes 16900
  114.6 120.8 %all-reduce.8.cloned.1.call-start = ((), (), s32[]{:S(2)}) async-start(), calls=%async_computation.3 | async-start | bytes 2162688 | tf_op jit(solution)/shard_map/psum | solution.py:103
  167.3 1.8 copy-start.3
  169.7 12.4 %copy-start.12 = (u32[32]{0:T(128)S(1)}, u32[32]{0:T(128)}, u32[]{:S(2)}) copy-start(u32[32]{0:T(128)} %constant.139) | copy-start | bytes 388
  169.7 13.6 %copy-start.8 = (s32[16]{0:T(128)S(1)}, s32[16]{0:T(128)}, u32[]{:S(2)}) copy-start(s32[16]{0:T(128)} %param.33) | copy-start | bytes 196
  169.7 65.6 %copy-start.6 = (f32[1408]{0:T(1024)S(1)}, f32[1408]{0:T(1024)}, u32[]{:S(2)}) copy-start(f32[1408]{0:T(1024)} %param.29) | copy-start | bytes 16900
  200.5 56.9 %copy-start.7 = (f32[1024]{0:T(1024)S(1)}, f32[1024]{0:T(1024)}, u32[]{:S(2)}) copy-start(f32[1024]{0:T(1024)} %param.31) | copy-start | bytes 12292
Sparse Core Ops, SparseCore 0:
  9.6 32.3 all-gather.3
  43.6 29.1 all-gather.5
  114.6 52.5 all-reduce.5
  182.2 53.1 all-reduce.7
where the time goes:
time: 271 us
  waiting for transfers between devices  137 us (51%)
  blocking collectives  47.1 us (17%)
  matrix products  38.9 us (14%)
  other arithmetic  21.6 us (8%)
  between operations  14.6 us (5%)
  local copies, waits for them, and re-layouts  10.5 us (4%)
    psum x1, waiting for transfers between devices, body(): lax.psum(attention_part.astype(jnp.bfloat16), 'head').astype(jnp.float32)  52.5 us
    psum x1, waiting for transfers between devices, body(): lax.psum(down_part.astype(jnp.bfloat16), 'head').astype(jnp.float32)  34.8 us
    all_gather x1, waiting for transfers between devices, body(): value_piece = lax.all_gather(values, 'blk', axis=0, tiled=True)  30.8 us
    all_gather x1, waiting for transfers between devices, body(): key_piece = lax.all_gather(keys, 'blk', axis=0, tiled=True)  18 us
    unnamed x1, blocking collectives  16.3 us
    pmax x1, blocking collectives, body(): global_request_max = lax.pmax(request_max, 'blk')  16.3 us
    all_gather x1, blocking collectives, body(): segment_piece = lax.all_gather(segment_wire, 'blk', axis=0, tiled=True)  14.4 us
    reduce_sum x3, other arithmetic, one_block(): jnp.sum(exponents, axis=-1)  13.5 us
  transfers between devices with their start and end apart: 4, of which 4 were waited for; matrix products, arithmetic and copies ran while one was open for 1% of the time, Pallas kernels for 0%

commit v1 on v0

v1 whole, which is shorter than its diff:
```python
import functools
import math

import jax
import jax.numpy as jnp
from jax import lax
from jax.experimental import pallas as pl
from jax.experimental.pallas import tpu as pltpu
from jax.sharding import PartitionSpec as P

HD = 88
NEGATIVE = -1e30
EPSILON = 1e-06
MESH = pl.DeviceIdType.MESH
F32 = jnp.float32
BF16 = jnp.bfloat16


def head_peer(me, k):
    y, x = me // 2, lax.rem(me, 2)
    return lax.rem(y + k // 2, 2) * 2 + lax.rem(x + lax.rem(k, 2), 2)


def nt_dot(a, b):
    return lax.dot_general(a, b, (((1,), (1,)), ((), ())), preferred_element_type=F32)


def layer_kernel(
    blk_count,
    att_ref,
    hid_ref,
    ob_ref,
    gain_ref,
    nb_ref,
    ub_ref,
    db_ref,
    mb_ref,
    slot_ref,
    lmax_ref,
    ow_hbm,
    up_hbm,
    dn_hbm,
    mg_hbm,
    out_ref,
    stat_ref,
    ow,
    up,
    dn,
    mg,
    psend,
    precv,
    nbuf,
    dsend,
    drecv,
    sbuf,
    mixed,
    merged,
    squares,
    gstat,
    load_sem,
    send_sem,
    recv_sem,
    stat_send,
    stat_recv,
):
    hg = lax.axis_index("head")
    blk = lax.axis_index("blk")
    groups = hid_ref.shape[0]
    width = hid_ref.shape[1]
    loads = [
        pltpu.make_async_copy(src, dst, load_sem.at[i])
        for i, (src, dst) in enumerate(((ow_hbm, ow), (up_hbm, up), (dn_hbm, dn), (mg_hbm, mg)))
    ]
    for load in loads:
        load.start()

    barrier = pltpu.get_barrier_semaphore()
    for k in (1, 2, 3):
        pl.semaphore_signal(barrier, inc=1, device_id={"head": head_peer(hg, k)}, device_id_type=MESH)

    def greet(i, carry):
        pl.semaphore_signal(
            barrier, inc=1, device_id={"blk": lax.rem(blk + i, blk_count)}, device_id_type=MESH
        )
        return carry

    lax.fori_loop(1, blk_count, greet, 0)
    pl.semaphore_wait(barrier, 3 + blk_count - 1)

    def exchange(phase, src, dst, k):
        return pltpu.make_async_remote_copy(
            src_ref=src,
            dst_ref=dst.at[k],
            send_sem=send_sem.at[phase, k],
            recv_sem=recv_sem.at[phase, k],
            device_id={"head": head_peer(hg, k)},
            device_id_type=MESH,
        )

    loads[0].wait()
    row = lax.broadcasted_iota(jnp.int32, (groups, 4 * groups), 0)
    col = lax.broadcasted_iota(jnp.int32, (groups, 4 * groups), 1)
    own = None
    for k in (3, 1, 2, 0):
        pick = jnp.where(col == 4 * row + head_peer(hg, k), 1.0, 0.0).astype(BF16)
        rows = nt_dot(pick, att_ref[...]).astype(BF16)
        term = jnp.dot(rows, ow[...], preferred_element_type=F32)
        if k == 0:
            own = term
        else:
            psend[k] = term.astype(BF16)
            exchange(0, psend.at[k], precv, k).start()
    total = hid_ref[...].astype(F32) + ob_ref[...] + own
    for k in (1, 2, 3):
        exchange(0, psend.at[k], precv, k).wait_recv()
        total = total + precv[k].astype(F32)
    mean = jnp.mean(total, axis=-1, keepdims=True)
    centered = total - mean
    var = jnp.mean(centered * centered, axis=-1, keepdims=True)
    nbuf[0] = (centered * lax.rsqrt(var + EPSILON) * gain_ref[...] + nb_ref[...]).astype(BF16)
    for k in (3, 1, 2):
        exchange(1, nbuf.at[0], nbuf, k).start()
    mixed[...] = total + db_ref[...]

    loads[1].wait()
    loads[2].wait()

    def mlp(k, carry):
        @pl.when(k > 0)
        def _():
            exchange(1, nbuf.at[0], nbuf, k).wait_recv()

        units = jnp.dot(nbuf[k], up[...], preferred_element_type=F32) + ub_ref[...]
        units = (0.5 * units * (1.0 + lax.erf(units * math.sqrt(0.5)))).astype(BF16)
        term = jnp.dot(units, dn[...], preferred_element_type=F32)

        @pl.when(k == 0)
        def _():
            mixed[...] += term

        @pl.when(k > 0)
        def _():
            dsend[k] = term.astype(BF16)
            exchange(2, dsend.at[k], drecv, k).start()

        return carry

    lax.fori_loop(0, 4, mlp, 0)

    state = mixed[...]
    for k in (1, 2, 3):
        exchange(2, dsend.at[k], drecv, k).wait_recv()
        state = state + drecv[k].astype(F32)
    sbuf[0] = state.astype(BF16)
    for k in (3, 1, 2):
        exchange(3, sbuf.at[0], sbuf, k).start()
    squares[...] = jnp.sum(state * state, axis=-1, keepdims=True)
    loads[3].wait()
    merged[...] = mb_ref[...] + jnp.dot(sbuf[0], mg[hg], preferred_element_type=F32)

    for k in (1, 2, 3):
        exchange(3, sbuf.at[0], sbuf, k).wait_recv()
        piece = sbuf[k].astype(F32)
        squares[...] += jnp.sum(piece * piece, axis=-1, keepdims=True)
    member = slot_ref[...] == lax.broadcasted_iota(jnp.int32, slot_ref.shape, 1)
    sums = jnp.sum(jnp.where(member, squares[...], 0.0), axis=0, keepdims=True)
    counts = jnp.sum(jnp.where(member, 4.0, 0.0), axis=0, keepdims=True)
    which = lax.broadcasted_iota(jnp.int32, lmax_ref.shape, 0)
    gstat[0] = jnp.where(which == 4, sums, jnp.where(which == 5, counts, lmax_ref[...]))

    def stat_copy(i):
        return pltpu.make_async_remote_copy(
            src_ref=gstat.at[0],
            dst_ref=gstat.at[i],
            send_sem=stat_send.at[i],
            recv_sem=stat_recv.at[i],
            device_id={"blk": lax.rem(blk + i, blk_count)},
            device_id_type=MESH,
        )

    def stat_start(i, carry):
        stat_copy(i).start()
        return carry

    lax.fori_loop(1, blk_count, stat_start, 0)

    def merge(k, carry):
        merged[...] += jnp.dot(sbuf[k], mg[head_peer(hg, k)], preferred_element_type=F32)
        return carry

    lax.fori_loop(1, 4, merge, 0)
    out_ref[...] = merged[...].astype(BF16)

    def stat_wait(i, carried):
        stat_copy(i).wait_recv()
        tile = gstat[i]
        return jnp.where(which < 4, jnp.maximum(carried, tile), carried + tile)

    tile = lax.fori_loop(1, blk_count, stat_wait, gstat[0])
    rms = jnp.sqrt(tile[4:5] / (jnp.maximum(tile[5:6], 1.0) * width) + EPSILON)
    stat_ref[...] = jnp.where(which == 4, rms, tile)

    for k in (1, 2, 3):
        exchange(0, psend.at[k], precv, k).wait_send()
        exchange(1, nbuf.at[0], nbuf, k).wait_send()
        exchange(2, dsend.at[k], drecv, k).wait_send()
        exchange(3, sbuf.at[0], sbuf, k).wait_send()

    def stat_sent(i, carry):
        stat_copy(i).wait_send()
        return carry

    lax.fori_loop(1, blk_count, stat_sent, 0)


def layer(att, hidden, out_bias, gain, nbias, ubias, dbias, mbias, slots, lmax, ow, up, dn, mg, n):
    groups, width = hidden.shape
    chunk = (4, groups, width)
    vmem = pl.BlockSpec(memory_space=pltpu.VMEM)
    hbm = pl.BlockSpec(memory_space=pl.ANY)
    return pl.pallas_call(
        functools.partial(layer_kernel, n),
        out_shape=(
            jax.ShapeDtypeStruct((groups, mg.shape[2]), BF16),
            jax.ShapeDtypeStruct(lmax.shape, F32),
        ),
        in_specs=[vmem] * 10 + [hbm] * 4,
        out_specs=(vmem, vmem),
        scratch_shapes=[
            pltpu.VMEM(ow.shape, BF16),
            pltpu.VMEM(up.shape, BF16),
            pltpu.VMEM(dn.shape, BF16),
            pltpu.VMEM(mg.shape, BF16),
            pltpu.VMEM(chunk, BF16),
            pltpu.VMEM(chunk, BF16),
            pltpu.VMEM(chunk, BF16),
            pltpu.VMEM(chunk, BF16),
            pltpu.VMEM(chunk, BF16),
            pltpu.VMEM(chunk, BF16),
            pltpu.VMEM((groups, width), F32),
            pltpu.VMEM((groups, mg.shape[2]), F32),
            pltpu.VMEM((groups, 1), F32),
            pltpu.VMEM((n,) + lmax.shape, F32),
            pltpu.SemaphoreType.DMA((4,)),
            pltpu.SemaphoreType.DMA((4, 4)),
            pltpu.SemaphoreType.DMA((4, 4)),
            pltpu.SemaphoreType.DMA((n,)),
            pltpu.SemaphoreType.DMA((n,)),
        ],
        compiler_params=pltpu.CompilerParams(
            collective_id=1, has_side_effects=True, vmem_limit_bytes=56 * 1024 * 1024
        ),
        name="layer",
    )(att, hidden, out_bias, gain, nbias, ubias, dbias, mbias, slots, lmax, ow, up, dn, mg)


def attention(queries, keys, values, row_segments):
    row_count = queries.shape[0]
    feat_width = queries.shape[1]
    head_count = feat_width // HD
    score_scale = HD ** (-0.5)
    segment_wire = row_segments.astype(jnp.bfloat16)
    segment_float = row_segments.astype(jnp.float32)
    query_heads = queries.reshape(row_count, head_count, HD)
    initial = (
        jnp.full((head_count, row_count), NEGATIVE, jnp.float32),
        jnp.zeros((head_count, row_count), jnp.float32),
        jnp.zeros((head_count, row_count, HD), jnp.float32),
    )
    key_piece = lax.all_gather(keys, "blk", axis=0, tiled=True)
    value_piece = lax.all_gather(values, "blk", axis=0, tiled=True)
    segment_piece = lax.all_gather(segment_wire, "blk", axis=0, tiled=True)
    piece_rows = key_piece.shape[0]
    key_block = math.gcd(piece_rows, 2048)

    def one_block(turn_index, carried):
        offset = turn_index * key_block
        block_keys = lax.dynamic_slice_in_dim(key_piece, offset, key_block, 0).reshape(
            key_block, head_count, HD
        )
        block_values = lax.dynamic_slice_in_dim(value_piece, offset, key_block, 0).reshape(
            key_block, head_count, HD
        )
        block_segments = lax.dynamic_slice_in_dim(segment_piece, offset, key_block, 0).astype(
            jnp.float32
        )
        old_max, old_sum, old_out = carried
        scores = (
            jnp.einsum("qhd,khd->hqk", query_heads, block_keys, preferred_element_type=jnp.float32)
            * score_scale
        )
        allowed = (segment_float[:, None] == block_segments[None, :])[None]
        scores = jnp.where(allowed, scores, NEGATIVE)
        new_max = jnp.maximum(old_max, jnp.max(scores, axis=-1))
        exponents = jnp.where(allowed, jnp.exp(scores - new_max[..., None]), 0.0)
        factor = jnp.exp(old_max - new_max)
        weights = exponents.astype(jnp.bfloat16)
        product = jnp.einsum(
            "hqk,khd->hqd", weights, block_values, preferred_element_type=jnp.float32
        )
        return (
            new_max,
            old_sum * factor + jnp.sum(exponents, axis=-1),
            old_out * factor[..., None] + product,
        )

    row_max, row_sum, row_out = lax.fori_loop(0, piece_rows // key_block, one_block, initial)
    attended = (
        jnp.transpose(row_out / row_sum[..., None], (0, 2, 1))
        .reshape(feat_width, row_count)
        .astype(jnp.bfloat16)
    )
    return attended, row_max


def body(
    hidden_in,
    queries,
    keys,
    values,
    out_weight,
    out_bias,
    norm_gain,
    norm_bias,
    up_weight,
    up_bias,
    down_weight,
    down_bias,
    merge_weight,
    merge_bias,
    group_segments,
    owner_slots,
):
    groups = group_segments.shape[0]
    model_width = hidden_in.shape[1]
    requests = owner_slots.shape[0]
    blk_count = lax.axis_size("blk")
    per_owner = requests // blk_count
    row_segments = jnp.repeat(group_segments, 4)
    attended, row_max = attention(queries, keys, values, row_segments)
    is_request = group_segments[:, None] == jnp.arange(requests, dtype=jnp.int32)[None, :]
    group_slots = jnp.sum(jnp.where(is_request, owner_slots[None, :], 0), axis=-1)
    row_slots = jnp.repeat(group_slots, 4)
    in_slot = row_slots[None, :] == jnp.arange(128, dtype=jnp.int32)[:, None]
    request_max = jnp.max(jnp.where(in_slot[None], row_max[:, None, :], NEGATIVE), axis=-1)
    lmax = jnp.pad(request_max, ((0, 8 - request_max.shape[0]), (0, 0)))
    hidden = lax.dynamic_index_in_dim(
        hidden_in.reshape(groups, 4, model_width), lax.axis_index("head"), 1, keepdims=False
    )
    merged_out, stats = layer(
        attended,
        hidden,
        out_bias[None],
        norm_gain[None],
        norm_bias[None],
        up_bias[None],
        down_bias[None],
        merge_bias[None],
        jnp.broadcast_to(group_slots[:, None], (groups, 128)),
        lmax,
        out_weight,
        up_weight,
        down_weight,
        merge_weight.reshape(4, model_width, -1),
        blk_count,
    )
    mine = lax.dynamic_slice_in_dim(stats, lax.axis_index("blk") * per_owner, per_owner, 1)
    return (merged_out, mine[4], jnp.transpose(mine[:4]))


def solution(mesh):
    in_specs = (
        P("blk", None),
        P("blk", "head"),
        P("blk", "head"),
        P("blk", "head"),
        P("head", None),
        P(),
        P(),
        P(),
        P(None, "head"),
        P("head"),
        P("head", None),
        P(),
        P(None, "head"),
        P("head"),
        P("blk"),
        P(),
    )
    out_specs = (P("blk", "head"), P("blk"), P("blk", "head"))
    return jax.shard_map(body, mesh=mesh, in_specs=in_specs, out_specs=out_specs, check_vma=False)
```

time: 271 us -> 193 us (0.71)
  waiting for transfers between devices: 137 us -> 40 us
  Pallas kernels: 0 us -> 65.4 us
  blocking collectives: 47.1 us -> 14.4 us
  matrix products: 38.9 us -> 20.9 us
  local copies, waits for them, and re-layouts: 10.5 us -> 19.5 us
  other arithmetic: 21.6 us -> 16.8 us
    psum x2 -> x0, waiting for transfers between devices: 87.3 us -> none  [the longest x1 52.5 us: body(): lax.psum(attention_part.astype(jnp.bfloat16), 'head').astype(jnp.float32)]
    pallas_call x0 -> x1, Pallas kernels: none -> 65.4 us  [layer(): pl.pallas_call(functools.partial(layer_kernel, n), out_shape=(jax.ShapeDt...]
    dot_general x3 -> x0, matrix products: 21 us -> none  [the longest x1 12.3 us: body(): jnp.dot(hidden_units, down_weight, preferred_element_type=jnp.float32)]
    unnamed x1 -> x0, blocking collectives: 16.3 us -> none
    pmax x1 -> x0, blocking collectives: 16.3 us -> none  [body(): global_request_max = lax.pmax(request_max, 'blk')]
    all_gather x2, waiting for transfers between devices: 48.8 us -> 38.6 us  [the longest x1 30.8 us: attention(): value_piece = lax.all_gather(values, 'blk', axis=0, tiled=True)]
    broadcast_in_dim x0 -> x7, local copies, waits for them, and re-layouts: none -> 7.23 us  [the longest x1 1.3 us: body(): norm_gain[None]]
    reduce_sum x5 -> x1, other arithmetic: 5.63 us -> 0.76 us  [body(): jnp.sum(jnp.where(is_request, owner_slots[None, :], 0), axis=-1)]
  transfers between devices with their start and end apart: 4 -> 2, of which waited for: 4 -> 2; matrix products, arithmetic and copies ran while one was open for 1% -> 6% of each run, Pallas kernels for 0% -> 0%
where the time goes in v1:
time: 193 us; the launch traced here: 191 us
  Pallas kernels  65.4 us (34%)
  waiting for transfers between devices  40 us (21%)
  matrix products  20.9 us (11%)
  local copies, waits for them, and re-layouts  19.5 us (10%)
  other arithmetic  16.8 us (9%)
  blocking collectives  14.4 us (7%)
  between operations  14.1 us (7%)
    pallas_call x1, Pallas kernels, layer(): pl.pallas_call(functools.partial(layer_kernel, n), out_shape=(jax.ShapeDt...  65.4 us
    all_gather x1, waiting for transfers between devices, attention(): value_piece = lax.all_gather(values, 'blk', axis=0, tiled=True)  30.8 us
    dot_general x3, matrix products, one_block(): jnp.einsum('qhd,khd->hqk', query_heads, block_keys, preferred_element_typ...  14.8 us
    all_gather x1, blocking collectives, attention(): segment_piece = lax.all_gather(segment_wire, 'blk', axis=0, tiled=True)  14.4 us
    reduce_sum x3, other arithmetic, one_block(): jnp.sum(exponents, axis=-1)  13.4 us
    all_gather x1, waiting for transfers between devices, attention(): key_piece = lax.all_gather(keys, 'blk', axis=0, tiled=True)  7.83 us
    dot_general x3, matrix products, one_block(): jnp.einsum('hqk,khd->hqd', weights, block_values, preferred_element_type=...  6.12 us
    dynamic_slice x3, local copies, waits for them, and re-layouts, one_block(): lax.dynamic_slice_in_dim(value_piece, offset, key_block, 0)  4.33 us
  transfers between devices with their start and end apart: 2, of which 2 were waited for; matrix products, arithmetic and copies ran while one was open for 6% of the time, Pallas kernels for 0%

profile of v1, /device:TPU:0, one launch (start us, length us, event | category | flops | bytes accessed | tf_op | source)
XLA Modules:
  0.0 191.4 jit_solution(2030460511417279050)
XLA Ops:
  7.2 0.0 all-gather.4.cloned.1.call-start
  7.2 0.7 all-gather.4.cloned.1.call-update
  7.9 0.0 all-gather.6.cloned.1.call-start
  7.9 0.7 all-gather.6.cloned.1.call-update
  8.7 0.7 fusion.15
  9.4 0.1 broadcast_in_dim.135
  9.5 0.1 reshape.95
  9.6 14.4 %all-gather = bf16[8,1,384]{2,1,0:T(2,128)(2,1)S(1)} all-gather(bf16[1,1,384]{2,1,0:T(2,128)(2,1)S(1)} %reshape.95), channel_id=1, replica_groups=mesh['head'=4,'blk'=8] {'blk'}, dimensions={0}, use_global_device_ids=true | all-gather | bytes 6912 | tf_op jit(solution)/shard_map/all_gather | solution.py:272
  24.0 1.4 reshape.93
  25.4 0.6 constant_dynamic-slice_fusion.3
  26.0 0.7 copy.34
  26.7 1.3 broadcast_in_dim.136.ob_ref
  28.0 1.3 broadcast_in_dim.137.gain_ref
  29.3 1.3 broadcast_in_dim.138.nb_ref
  30.6 1.3 broadcast_in_dim.139.ub_ref
  31.9 1.3 broadcast_in_dim.140.db_ref
  33.2 0.8 select_reduce_fusion.1
  33.9 0.1 broadcast_in_dim.145
  34.0 0.1 eq.68
  34.2 7.8 %all-gather.4.cloned.1.call-done = bf16[3072,352]{0,1:T(8,128)(2,1)} async-done(((bf16[384,352]{0,1:T(8,128)(2,1)}), bf16[3072,352]{0,1:T(8,128)(2,1)}) %all-gather.4.cloned.1.call-update) | async-done | bytes 2162704 | tf_op jit(solution)/shard_map/all_gather | solution.py:270
  42.0 30.8 %all-gather.6.cloned.1.call-done = bf16[3072,352]{0,1:T(8,128)(2,1)} async-done(((bf16[384,352]{0,1:T(8,128)(2,1)}), bf16[3072,352]{0,1:T(8,128)(2,1)}) %all-gather.6.cloned.1.call-update) | async-done | bytes 2162704 | tf_op jit(solution)/shard_map/all_gather | solution.py:271
  72.8 40.6 %while.18 = (s32[]{:T(128)}, f32[4,384]{1,0:T(4,128)S(1)}, f32[4,384]{1,0:T(4,128)S(1)}, f32[4,384,88]{1,2,0:T(8,128)S(1)}, bf16[3072]{0:T(1024)(128)(2,1)S(1)},...) while((s32[]{:T(128)}, f32[4,384]{1,0:T(4,128)S(1)}, ...), condition=%wide.region_3.4_spmd.clone, body=%wide.region_0.3_spmd.clone.sunk | while | flops 574902784 | bytes 51405408 | solution.py:307
  72.8 0.1 broadcast_in_dim.197
  72.9 0.1 convert_element_type.63
  73.0 0.3 broadcast_compare_fusion.2
  73.3 1.4 constant_dynamic-slice_fusion.5
  74.7 4.9 %fusion.31 = (f32[4,384]{1,0:T(4,128)S(1)}, f32[4,1024,384]{2,1,0:T(8,128)}) fusion(pred[384,1024]{0,1:T(8,128)(4,1)S(1)} %broadcast_compare_fusion.2, bf16[1024,4,88]{0,2,1:T(8,128)(2,1)S(1)} %bitcast.47, bf16[384,4,88]{0,2,1:T(8,128)(2,1)} %get-tuple-element.336), kind=kOutput, calls=%fused_computation.3.clone.1 | convolution fusion | flops 281541120 | bytes 7682048 | tf_op jit(solution)/shard_map/while/body/eval_jaxpr/qhd,khd->hqk/dot_general | solution.py:289
  79.7 0.0 copy-start
  79.7 4.5 %fusion.32 = f32[4,384]{1,0:T(4,128)S(1)} fusion(f32[4,1024,384]{2,1,0:T(8,128)} %get-tuple-element.300, f32[4,384]{1,0:T(4,128)S(1)} %select_maximum_fusion.2, pred[384,1024]{0,1:T(8,128)(4,1)S(1)} %broadcast_compare_fusion.2), kind=kLoop, calls=%fused_computation.5.clone.1 | loop fusion | flops 7862784 | bytes 6696960 | tf_op jit(solution)/shard_map/while/body/eval_jaxpr/reduce_sum | solution.py:303
  84.2 0.1 copy-done
  84.3 2.0 %fusion.34 = f32[4,384,88]{1,2,0:T(8,128)S(1)} fusion(bf16[1024,4,88]{0,2,1:T(8,128)(2,1)S(1)} %bitcast.48, f32[4,1024,384]{2,1,0:T(8,128)S(1)} %copy-done, f32[4,384]{1,0:T(4,128)S(1)} %select_maximum_fusion.2, pred[384,1024]{0,1:T(8,128)(4,1)S(1)} %broadcast_compare_fusion.2, f32[4,384,88]{1,2,0:T(8,128)S(1)} %get-tuple-element.320, ...), kind=kOutput, calls=%fused_computation.8.clone.1 | convolution fusion | flops 285093888 | bytes 8499201 | tf_op jit(solution)/shard_map/while/body/eval_jaxpr/hqk,khd->hqd/dot_general | solution.py:298
  86.3 0.1 broadcast_in_dim.197
  86.4 0.1 convert_element_type.63
  86.5 0.3 broadcast_compare_fusion.2
  86.8 1.4 constant_dynamic-slice_fusion.5
  88.3 4.9 %fusion.31 = (f32[4,384]{1,0:T(4,128)S(1)}, f32[4,1024,384]{2,1,0:T(8,128)}) fusion(pred[384,1024]{0,1:T(8,128)(4,1)S(1)} %broadcast_compare_fusion.2, bf16[1024,4,88]{0,2,1:T(8,128)(2,1)S(1)} %bitcast.47, bf16[384,4,88]{0,2,1:T(8,128)(2,1)} %get-tuple-element.336), kind=kOutput, calls=%fused_computation.3.clone.1 | convolution fusion | flops 281541120 | bytes 7682048 | tf_op jit(solution)/shard_map/while/body/eval_jaxpr/qhd,khd->hqk/dot_general | solution.py:289
  93.2 0.0 copy-start
  93.2 4.5 %fusion.32 = f32[4,384]{1,0:T(4,128)S(1)} fusion(f32[4,1024,384]{2,1,0:T(8,128)} %get-tuple-element.300, f32[4,384]{1,0:T(4,128)S(1)} %select_maximum_fusion.2, pred[384,1024]{0,1:T(8,128)(4,1)S(1)} %broadcast_compare_fusion.2), kind=kLoop, calls=%fused_computation.5.clone.1 | loop fusion | flops 7862784 | bytes 6696960 | tf_op jit(solution)/shard_map/while/body/eval_jaxpr/reduce_sum | solution.py:303
  97.7 0.1 copy-done
  97.8 2.0 %fusion.34 = f32[4,384,88]{1,2,0:T(8,128)S(1)} fusion(bf16[1024,4,88]{0,2,1:T(8,128)(2,1)S(1)} %bitcast.48, f32[4,1024,384]{2,1,0:T(8,128)S(1)} %copy-done, f32[4,384]{1,0:T(4,128)S(1)} %select_maximum_fusion.2, pred[384,1024]{0,1:T(8,128)(4,1)S(1)} %broadcast_compare_fusion.2, f32[4,384,88]{1,2,0:T(8,128)S(1)} %get-tuple-element.320, ...), kind=kOutput, calls=%fused_computation.8.clone.1 | convolution fusion | flops 285093888 | bytes 8499201 | tf_op jit(solution)/shard_map/while/body/eval_jaxpr/hqk,khd->hqd/dot_general | solution.py:298
  99.8 0.1 broadcast_in_dim.197
  99.9 0.1 convert_element_type.63
  100.1 0.3 broadcast_compare_fusion.2
  100.3 1.4 constant_dynamic-slice_fusion.5
  101.8 4.9 %fusion.31 = (f32[4,384]{1,0:T(4,128)S(1)}, f32[4,1024,384]{2,1,0:T(8,128)}) fusion(pred[384,1024]{0,1:T(8,128)(4,1)S(1)} %broadcast_compare_fusion.2, bf16[1024,4,88]{0,2,1:T(8,128)(2,1)S(1)} %bitcast.47, bf16[384,4,88]{0,2,1:T(8,128)(2,1)} %get-tuple-element.336), kind=kOutput, calls=%fused_computation.3.clone.1 | convolution fusion | flops 281541120 | bytes 7682048 | tf_op jit(solution)/shard_map/while/body/eval_jaxpr/qhd,khd->hqk/dot_general | solution.py:289
  106.7 0.0 copy-start
  106.7 4.5 %fusion.32 = f32[4,384]{1,0:T(4,128)S(1)} fusion(f32[4,1024,384]{2,1,0:T(8,128)} %get-tuple-element.300, f32[4,384]{1,0:T(4,128)S(1)} %select_maximum_fusion.2, pred[384,1024]{0,1:T(8,128)(4,1)S(1)} %broadcast_compare_fusion.2), kind=kLoop, calls=%fused_computation.5.clone.1 | loop fusion | flops 7862784 | bytes 6696960 | tf_op jit(solution)/shard_map/while/body/eval_jaxpr/reduce_sum | solution.py:303
  111.2 0.1 copy-done
  111.3 2.0 %fusion.34 = f32[4,384,88]{1,2,0:T(8,128)S(1)} fusion(bf16[1024,4,88]{0,2,1:T(8,128)(2,1)S(1)} %bitcast.48, f32[4,1024,384]{2,1,0:T(8,128)S(1)} %copy-done, f32[4,384]{1,0:T(4,128)S(1)} %select_maximum_fusion.2, pred[384,1024]{0,1:T(8,128)(4,1)S(1)} %broadcast_compare_fusion.2, f32[4,384,88]{1,2,0:T(8,128)S(1)} %get-tuple-element.320, ...), kind=kOutput, calls=%fused_computation.8.clone.1 | convolution fusion | flops 285093888 | bytes 8499201 | tf_op jit(solution)/shard_map/while/body/eval_jaxpr/hqk,khd->hqd/dot_general | solution.py:298
  113.4 0.7 divide_convert_fusion
  114.1 0.2 select_reduce_fusion
  114.3 0.6 pad.4.lmax_ref
  114.9 0.7 broadcast_in_dim.144.slot_ref
  115.6 65.4 %layer.1 = (bf16[96,1024]{1,0:T(8,128)(2,1)}, f32[8,128]{1,0:T(8,128)}) custom-call(bf16[352,384]{1,0:T(8,128)(2,1)} %bitcast.52, bf16[96,1408]{1,0:T(8,128)(2,1)} %bitcast.51, f32[1,1408]{1,0:T(1,128)} %broadcast_in_dim.136.ob_ref, f32[1,1408]{1,0:T(1,128)} %broadcast_in_dim.137.gain_ref, f32[1,1408]{1,0:T(1,128)} %broadcast_in_dim.138.nb_ref, ...), custom_call_target="tpu_custom_call" | custom-call | tf_op jit(solution)/shard_map/layer/pallas_call | solution.py:221
  181.0 0.8 constant_dynamic-slice_fusion.2
  181.8 0.5 slice_bitcast_fusion.1
  182.3 0.7 copy.30
  182.9 1.6 copy.48
  (19 shorter events, 0.2 us)
Async XLA Ops:
  7.2 34.8 %all-gather.4.cloned.1.call-start = ((), (), s32[]{:S(2)}) async-start(), calls=%async_computation | async-start | bytes 2433024 | tf_op jit(solution)/shard_map/all_gather | solution.py:270
  7.9 64.9 %all-gather.6.cloned.1.call-start = ((), (), s32[]{:S(2)}) async-start(), calls=%async_computation.1 | async-start | bytes 2433024 | tf_op jit(solution)/shard_map/all_gather | solution.py:271
  79.7 4.6 %copy-start = (f32[4,1024,384]{2,1,0:T(8,128)S(1)}, f32[4,1024,384]{2,1,0:T(8,128)}, u32[]{:S(2)}) copy-start(f32[4,1024,384]{2,1,0:T(8,128)} %get-tuple-element.300) | copy-start | bytes 18874372 | tf_op jit(solution)/shard_map/while
  93.2 4.6 %copy-start = (f32[4,1024,384]{2,1,0:T(8,128)S(1)}, f32[4,1024,384]{2,1,0:T(8,128)}, u32[]{:S(2)}) copy-start(f32[4,1024,384]{2,1,0:T(8,128)} %get-tuple-element.300) | copy-start | bytes 18874372 | tf_op jit(solution)/shard_map/while
  106.7 4.6 %copy-start = (f32[4,1024,384]{2,1,0:T(8,128)S(1)}, f32[4,1024,384]{2,1,0:T(8,128)}, u32[]{:S(2)}) copy-start(f32[4,1024,384]{2,1,0:T(8,128)} %get-tuple-element.300) | copy-start | bytes 18874372 | tf_op jit(solution)/shard_map/while
Sparse Core Ops, SparseCore 0:
  9.6 32.3 all-gather.3
  43.6 29.1 all-gather.5

commit v2 on v1

v2 whole, which is shorter than its diff:
```python
import functools
import math

import jax
import jax.numpy as jnp
from jax import lax
from jax.experimental import pallas as pl
from jax.experimental.pallas import tpu as pltpu
from jax.sharding import PartitionSpec as P

HD = 88
NEGATIVE = -1e30
EPSILON = 1e-06
ROWS = 96
CODE = 72.0
MESH = pl.DeviceIdType.MESH
F32 = jnp.float32
BF16 = jnp.bfloat16


def head_peer(me, k):
    y, x = me // 2, lax.rem(me, 2)
    return lax.rem(y + k // 2, 2) * 2 + lax.rem(x + lax.rem(k, 2), 2)


def nt_dot(a, b):
    return lax.dot_general(a, b, (((1,), (1,)), ((), ())), preferred_element_type=F32)


def nn_dot(a, b):
    return jnp.dot(a, b, preferred_element_type=F32)


def layer_kernel(
    blk_count,
    parts,
    requests,
    q_ref,
    k_ref,
    v_ref,
    seg_ref,
    hid_ref,
    ob_ref,
    gain_ref,
    nb_ref,
    ub_ref,
    db_ref,
    mb_ref,
    ow_hbm,
    up_hbm,
    dn_hbm,
    mg_hbm,
    out_ref,
    stat_ref,
    ow,
    up,
    dn,
    mg,
    owp,
    xsend,
    x,
    scores,
    asend,
    att,
    psend,
    precv,
    nbuf,
    dsend,
    drecv,
    sbuf,
    mixed,
    merged,
    squares,
    gstat,
    load_sem,
    send_sem,
    recv_sem,
    stat_send,
    stat_recv,
    pass_send,
    pass_recv,
):
    hg = lax.axis_index("head")
    blk = lax.axis_index("blk")
    tokens, width = hid_ref.shape
    groups = tokens // 4
    mine = blk // parts
    part = lax.rem(blk, parts)
    loads = [
        pltpu.make_async_copy(src, dst, load_sem.at[i])
        for i, (src, dst) in enumerate(((ow_hbm, ow), (up_hbm, up), (dn_hbm, dn), (mg_hbm, mg)))
    ]
    for load in loads:
        load.start()

    barrier = pltpu.get_barrier_semaphore()
    for k in (1, 2, 3):
        pl.semaphore_signal(barrier, inc=1, device_id={"head": head_peer(hg, k)}, device_id_type=MESH)

    def greet(i, carry):
        pl.semaphore_signal(
            barrier, inc=1, device_id={"blk": lax.rem(blk + i, blk_count)}, device_id_type=MESH
        )
        return carry

    lax.fori_loop(1, blk_count, greet, 0)

    def exchange(phase, src, dst, k):
        return pltpu.make_async_remote_copy(
            src_ref=src,
            dst_ref=dst.at[k],
            send_sem=send_sem.at[phase, k],
            recv_sem=recv_sem.at[phase, k],
            device_id={"head": head_peer(hg, k)},
            device_id_type=MESH,
        )

    def scatter(i):
        goal = lax.rem(mine + i, 4)
        return pltpu.make_async_remote_copy(
            src_ref=xsend.at[goal],
            dst_ref=x.at[blk],
            send_sem=send_sem.at[4, i],
            recv_sem=recv_sem.at[4, i],
            device_id={"blk": goal * parts + part},
            device_id_type=MESH,
        )

    def give_back(i):
        goal = lax.rem(mine + i, 4)
        return pltpu.make_async_remote_copy(
            src_ref=asend.at[goal],
            dst_ref=att.at[pl.ds(pl.multiple_of(mine * ROWS, ROWS), ROWS)],
            send_sem=send_sem.at[5, i],
            recv_sem=recv_sem.at[5, i],
            device_id={"blk": goal * parts + part},
            device_id_type=MESH,
        )

    def hand_on(i, j):
        held = lax.rem(mine + 4 - i, 4) * parts + part
        return pltpu.make_async_remote_copy(
            src_ref=x.at[held, pl.ds(0, 2)],
            dst_ref=x.at[held, pl.ds(0, 2)],
            send_sem=pass_send.at[i, j],
            recv_sem=pass_recv.at[i, j],
            device_id={"blk": mine * parts + lax.rem(part + j, parts)},
            device_id_type=MESH,
        )

    seg = jnp.broadcast_to(seg_ref[...], (8, groups))
    spread = jnp.where(
        lax.broadcasted_iota(jnp.int32, (groups, tokens), 1) // 4
        == lax.broadcasted_iota(jnp.int32, (groups, tokens), 0),
        1.0,
        0.0,
    ).astype(BF16)
    row_seg = nn_dot(seg.astype(F32).astype(BF16), spread).astype(jnp.int32)
    code_row = lax.broadcasted_iota(jnp.int32, (8, tokens), 0)
    bits = (requests - 1).bit_length()
    code = jnp.where(lax.shift_right_logical(row_seg, code_row) % 2 == 1, CODE, -CODE)
    code = jnp.where(code_row < bits, code, 0.0)
    ones = jnp.where(code_row == 0, 1.0, 0.0)
    for slot, (ref, tail) in enumerate(((k_ref, code), (v_ref, ones), (q_ref, code))):
        whole = ref[...].astype(F32)
        for h in range(4):
            piece = jnp.concatenate([whole[h * HD : (h + 1) * HD], tail], axis=0)
            xsend[h, slot] = piece.astype(BF16)

    pl.semaphore_wait(barrier, 3 + blk_count - 1)
    for i in (2, 1, 3):
        scatter(i).start()
    x[blk] = xsend[mine]

    def pass_all(i):
        def one(j, carry):
            hand_on(i, j).start()
            return carry

        lax.fori_loop(1, parts, one, 0)

    pass_all(0)
    loads[0].wait()
    whole = ow[...].astype(F32)
    for h in range(4):
        padded = jnp.concatenate(
            [whole[h * HD : (h + 1) * HD], jnp.zeros((ROWS - HD, width), F32)], axis=0
        )
        owp[h * ROWS : (h + 1) * ROWS] = padded.astype(BF16)
    for i in (1, 3, 2):
        scatter(i).wait_recv()
        pass_all(i)
    for i in range(4):

        def landed(j, carry):
            hand_on(i, j).wait_recv()
            return carry

        lax.fori_loop(1, parts, landed, 0)

    rate = HD ** (-0.5)
    speed = rate * math.log2(math.e)
    shift = bits * CODE * CODE
    tile = scores.shape[2]
    names = lax.broadcasted_iota(jnp.int32, (requests, tile), 0).astype(F32)
    weights_of = jnp.where(
        lax.broadcasted_iota(jnp.int32, (8, tile), 0) < bits,
        lax.shift_left(1, lax.broadcasted_iota(jnp.int32, (8, tile), 0)).astype(F32),
        0.0,
    )
    top = jnp.full((requests, 1), NEGATIVE, F32)
    for i in (2, 1, 3, 0):
        goal = lax.rem(mine + i, 4)
        for at in range(0, tokens, tile):
            query = x[goal * parts + part, 2, :, at : at + tile]

            def score(b, best):
                got = lax.dot_general(
                    x[b, 0], query, (((0,), (0,)), ((), ())), preferred_element_type=F32
                )
                scores[b] = got
                return jnp.maximum(best, jnp.max(got, axis=0, keepdims=True))

            best = lax.fori_loop(
                0, blk_count, score, jnp.full((1, tile), NEGATIVE, F32), unroll=4
            )
            base = best * speed

            def blend(b, total):
                weight = jnp.exp2(scores[b] * speed - base).astype(BF16)
                return total + nn_dot(x[b, 1], weight)

            total = lax.fori_loop(0, blk_count, blend, jnp.zeros((ROWS, tile), F32), unroll=4)
            asend[goal, :, at : at + tile] = (total / total[HD : HD + 1]).astype(BF16)
            marks = query.astype(F32)[HD:ROWS]
            name = jnp.sum(jnp.where(marks > 0, weights_of, 0.0), axis=0, keepdims=True)
            inside = jnp.where(names == name, (best - shift) * rate, NEGATIVE)
            top = jnp.maximum(top, jnp.max(inside, axis=1, keepdims=True))
        if i > 0:
            give_back(i).start()
    att[pl.ds(pl.multiple_of(mine * ROWS, ROWS), ROWS)] = asend[mine]

    row = lax.broadcasted_iota(jnp.int32, (groups, tokens), 0)
    col = lax.broadcasted_iota(jnp.int32, (groups, tokens), 1)

    def pick(k):
        return jnp.where(col == 4 * row + head_peer(hg, k), 1.0, 0.0).astype(BF16)

    total = nn_dot(pick(0), hid_ref[...]) + ob_ref[...]
    for i in (1, 2, 3):
        give_back(i).wait_recv()
    for k in (3, 1, 2, 0):
        rows = nt_dot(pick(k), att[...]).astype(BF16)
        term = nn_dot(rows, owp[...])
        if k == 0:
            total = total + term
        else:
            psend[k] = term.astype(BF16)
            exchange(0, psend.at[k], precv, k).start()
    for k in (1, 2, 3):
        exchange(0, psend.at[k], precv, k).wait_recv()
        total = total + precv[k].astype(F32)
    mean = jnp.mean(total, axis=-1, keepdims=True)
    centered = total - mean
    var = jnp.mean(centered * centered, axis=-1, keepdims=True)
    nbuf[0] = (centered * lax.rsqrt(var + EPSILON) * gain_ref[...] + nb_ref[...]).astype(BF16)
    for k in (3, 1, 2):
        exchange(1, nbuf.at[0], nbuf, k).start()
    mixed[...] = total + db_ref[...]

    loads[1].wait()
    loads[2].wait()

    def mlp(k, carry):
        @pl.when(k > 0)
        def _():
            exchange(1, nbuf.at[0], nbuf, k).wait_recv()

        units = nn_dot(nbuf[k], up[...]) + ub_ref[...]
        units = (0.5 * units * (1.0 + lax.erf(units * math.sqrt(0.5)))).astype(BF16)
        term = nn_dot(units, dn[...])

        @pl.when(k == 0)
        def _():
            mixed[...] += term

        @pl.when(k > 0)
        def _():
            dsend[k] = term.astype(BF16)
            exchange(2, dsend.at[k], drecv, k).start()

        return carry

    lax.fori_loop(0, 4, mlp, 0)

    state = mixed[...]
    for k in (1, 2, 3):
        exchange(2, dsend.at[k], drecv, k).wait_recv()
        state = state + drecv[k].astype(F32)
    sbuf[0] = state.astype(BF16)
    for k in (3, 1, 2):
        exchange(3, sbuf.at[0], sbuf, k).start()
    squares[...] = jnp.sum(state * state, axis=-1, keepdims=True)
    loads[3].wait()
    merged[...] = mb_ref[...] + nn_dot(sbuf[0], mg[hg])

    for k in (1, 2, 3):
        exchange(3, sbuf.at[0], sbuf, k).wait_recv()
        piece = sbuf[k].astype(F32)
        squares[...] += jnp.sum(piece * piece, axis=-1, keepdims=True)
    ids = lax.broadcasted_iota(jnp.int32, (requests, groups), 0)
    member = jnp.where(seg_ref[...] == ids, 1.0, 0.0)
    sums = jnp.dot(
        member,
        jnp.broadcast_to(squares[...], (groups, 128)),
        preferred_element_type=F32,
        precision=lax.Precision.HIGHEST,
    )
    counts = 4.0 * jnp.sum(member, axis=1, keepdims=True)
    lane = lax.broadcasted_iota(jnp.int32, (requests, 128), 1)
    gstat[0] = jnp.where(lane == 0, top, jnp.where(lane == 1, sums, counts))

    def stat_copy(i):
        return pltpu.make_async_remote_copy(
            src_ref=gstat.at[0],
            dst_ref=gstat.at[i],
            send_sem=stat_send.at[i],
            recv_sem=stat_recv.at[i],
            device_id={"blk": lax.rem(blk + i, blk_count)},
            device_id_type=MESH,
        )

    def stat_start(i, carry):
        stat_copy(i).start()
        return carry

    lax.fori_loop(1, blk_count, stat_start, 0)

    def merge(k, carry):
        merged[...] += nn_dot(sbuf[k], mg[head_peer(hg, k)])
        return carry

    lax.fori_loop(1, 4, merge, 0)
    out_ref[...] = merged[...].astype(BF16)

    def fold(i, carry):
        added, best = carry
        got = gstat[i]
        source = lax.rem(blk + blk_count - i, blk_count) // parts
        return added + got, jnp.maximum(best, jnp.where(lane == 8 + source, got[:, 0:1], NEGATIVE))

    def stat_wait(i, carry):
        stat_copy(i).wait_recv()
        return fold(i, carry)

    start = (jnp.zeros((requests, 128), F32), jnp.full((requests, 128), NEGATIVE, F32))
    added, best = lax.fori_loop(1, blk_count, stat_wait, fold(0, start))
    rms = jnp.sqrt(added[:, 1:2] / (jnp.maximum(added[:, 2:3], 1.0) * width) + EPSILON)
    stat_ref[...] = jnp.where(lane == 1, rms, best)

    for k in (1, 2, 3):
        scatter(k).wait_send()
        give_back(k).wait_send()
        exchange(0, psend.at[k], precv, k).wait_send()
        exchange(1, nbuf.at[0], nbuf, k).wait_send()
        exchange(2, dsend.at[k], drecv, k).wait_send()
        exchange(3, sbuf.at[0], sbuf, k).wait_send()
    for i in range(4):

        def passed(j, carry):
            hand_on(i, j).wait_send()
            return carry

        lax.fori_loop(1, parts, passed, 0)

    def stat_sent(i, carry):
        stat_copy(i).wait_send()
        return carry

    lax.fori_loop(1, blk_count, stat_sent, 0)


def layer(operands, weights, n, requests):
    tokens, width = operands[4].shape
    groups = tokens // 4
    parts = n // 4
    ow, up, dn, mg = weights
    chunk = pltpu.VMEM((4, groups, width), BF16)
    tile = tokens if n <= 8 else tokens // 3
    vmem = pl.BlockSpec(memory_space=pltpu.VMEM)
    hbm = pl.BlockSpec(memory_space=pl.ANY)
    return pl.pallas_call(
        functools.partial(layer_kernel, n, parts, requests),
        out_shape=(
            jax.ShapeDtypeStruct((groups, mg.shape[2]), BF16),
            jax.ShapeDtypeStruct((requests, 128), F32),
        ),
        in_specs=[vmem] * len(operands) + [hbm] * 4,
        out_specs=(vmem, vmem),
        scratch_shapes=[
            pltpu.VMEM(ow.shape, BF16),
            pltpu.VMEM(up.shape, BF16),
            pltpu.VMEM(dn.shape, BF16),
            pltpu.VMEM(mg.shape, BF16),
            pltpu.VMEM((4 * ROWS, width), BF16),
            pltpu.VMEM((4, 3, ROWS, tokens), BF16),
            pltpu.VMEM((n, 3, ROWS, tokens), BF16),
            pltpu.VMEM((n, tokens, tile), F32),
            pltpu.VMEM((4, ROWS, tokens), BF16),
            pltpu.VMEM((4 * ROWS, tokens), BF16),
            chunk,
            chunk,
            chunk,
            chunk,
            chunk,
            chunk,
            pltpu.VMEM((groups, width), F32),
            pltpu.VMEM((groups, mg.shape[2]), F32),
            pltpu.VMEM((groups, 1), F32),
            pltpu.VMEM((n, requests, 128), F32),
            pltpu.SemaphoreType.DMA((4,)),
            pltpu.SemaphoreType.DMA((6, 4)),
            pltpu.SemaphoreType.DMA((6, 4)),
            pltpu.SemaphoreType.DMA((n,)),
            pltpu.SemaphoreType.DMA((n,)),
            pltpu.SemaphoreType.DMA((4, parts)),
            pltpu.SemaphoreType.DMA((4, parts)),
        ],
        compiler_params=pltpu.CompilerParams(
            collective_id=1, has_side_effects=True, vmem_limit_bytes=58 * 1024 * 1024
        ),
        name="layer",
    )(*operands, *weights)


def body(
    hidden_in,
    queries,
    keys,
    values,
    out_weight,
    out_bias,
    norm_gain,
    norm_bias,
    up_weight,
    up_bias,
    down_weight,
    down_bias,
    merge_weight,
    merge_bias,
    group_segments,
    owner_slots,
):
    model_width = hidden_in.shape[1]
    requests = owner_slots.shape[0]
    blk_count = lax.axis_size("blk")
    per_owner = requests // blk_count
    merged_out, stats = layer(
        (
            queries.T,
            keys.T,
            values.T,
            group_segments[None],
            hidden_in,
            out_bias[None],
            norm_gain[None],
            norm_bias[None],
            up_bias[None],
            down_bias[None],
            merge_bias[None],
        ),
        (out_weight, up_weight, down_weight, merge_weight.reshape(4, model_width, -1)),
        blk_count,
        requests,
    )
    slot_ids = lax.axis_index("blk") * per_owner + jnp.arange(per_owner, dtype=jnp.int32)
    mine = owner_slots[None, :] == slot_ids[:, None]
    picked = jnp.sum(jnp.where(mine[:, :, None], stats[None, :, :16], 0.0), axis=1)
    return (merged_out, picked[:, 1], picked[:, 8:12])


def solution(mesh):
    in_specs = (
        P("blk", None),
        P("blk", "head"),
        P("blk", "head"),
        P("blk", "head"),
        P("head", None),
        P(),
        P(),
        P(),
        P(None, "head"),
        P("head"),
        P("head", None),
        P(),
        P(None, "head"),
        P("head"),
        P("blk"),
        P(),
    )
    out_specs = (P("blk", "head"), P("blk"), P("blk", "head"))
    return jax.shard_map(body, mesh=mesh, in_specs=in_specs, out_specs=out_specs, check_vma=False)
```

time: 193 us -> 114 us (0.59)
  waiting for transfers between devices: 40 us -> 0 us
  Pallas kernels: 65.4 us -> 102 us
  matrix products: 20.9 us -> 0 us
  other arithmetic: 16.8 us -> 0.86 us
  blocking collectives: 14.4 us -> 0 us
  between operations: 14.1 us -> 0.66 us
  local copies, waits for them, and re-layouts: 19.5 us -> 9.41 us
    all_gather x2 -> x0, waiting for transfers between devices: 38.6 us -> none  [the longest x1 30.8 us: attention(): value_piece = lax.all_gather(values, 'blk', axis=0, tiled=True)]
    pallas_call x1, Pallas kernels: 65.4 us -> 102 us  [layer(): pl.pallas_call(functools.partial(layer_kernel, n, parts, requests), out_s...]
    dot_general x6 -> x0, matrix products: 20.9 us -> none  [the longest x3 14.8 us: one_block(): jnp.einsum('qhd,khd->hqk', query_heads, block_keys, preferred_element_typ...]
    all_gather x1 -> x0, blocking collectives: 14.4 us -> none  [attention(): segment_piece = lax.all_gather(segment_wire, 'blk', axis=0, tiled=True)]
    reduce_sum x4 -> x1, other arithmetic: 14.2 us -> 0.78 us  [body(): jnp.sum(jnp.where(mine[:, :, None], stats[None, :, :16], 0.0), axis=1)]
    dynamic_slice x5 -> x0, local copies, waits for them, and re-layouts: 5.65 us -> none  [the longest x3 4.33 us: one_block(): lax.dynamic_slice_in_dim(value_piece, offset, key_block, 0)]
  transfers between devices with their start and end apart: 2 -> 0, of which waited for: 2 -> 0; matrix products, arithmetic and copies ran while one was open for 6% -> 0% of each run, Pallas kernels for 0% -> 0%
where the time goes in v2:
time: 114 us; the launch traced here: 113 us
  Pallas kernels  102 us (89%)
  local copies, waits for them, and re-layouts  9.41 us (8%)
    pallas_call x1, Pallas kernels, layer(): pl.pallas_call(functools.partial(layer_kernel, n, parts, requests), out_s...  102 us

profile of v2, /device:TPU:0, one launch (start us, length us, event | category | flops | bytes accessed | tf_op | source)
XLA Modules:
  0.0 112.5 jit_solution(8382142150081786413)
XLA Ops:
  0.6 1.3 %broadcast_in_dim.49.ub_ref = f32[1,1536]{1,0:T(1,128)} reshape(f32[1536]{0:T(1024)} %param.25) | data formatting | bytes 12288 | tf_op jit(solution)/shard_map/broadcast_in_dim | solution.py:468
  1.9 1.3 %broadcast_in_dim.46.ob_ref = f32[1,1408]{1,0:T(1,128)} reshape(f32[1408]{0:T(1024)} %param.21) | data formatting | bytes 11264 | tf_op jit(solution)/shard_map/broadcast_in_dim | solution.py:465
  3.2 1.3 %broadcast_in_dim.47.gain_ref = f32[1,1408]{1,0:T(1,128)} reshape(f32[1408]{0:T(1024)} %param.22) | data formatting | bytes 11264 | tf_op jit(solution)/shard_map/broadcast_in_dim | solution.py:466
  4.5 1.3 %broadcast_in_dim.48.nb_ref = f32[1,1408]{1,0:T(1,128)} reshape(f32[1408]{0:T(1024)} %param.23) | data formatting | bytes 11264 | tf_op jit(solution)/shard_map/broadcast_in_dim | solution.py:467
  5.8 1.3 %broadcast_in_dim.50.db_ref = f32[1,1408]{1,0:T(1,128)} reshape(f32[1408]{0:T(1024)} %param.27) | data formatting | bytes 11264 | tf_op jit(solution)/shard_map/broadcast_in_dim | solution.py:469
  7.1 0.0 copy-start
  7.1 101.6 %layer.1 = (bf16[96,1024]{1,0:T(8,128)(2,1)}, f32[16,128]{1,0:T(8,128)}) custom-call(bf16[352,384]{1,0:T(8,128)(2,1)} %bitcast.8, bf16[352,384]{1,0:T(8,128)(2,1)} %bitcast.9, bf16[352,384]{1,0:T(8,128)(2,1)} %bitcast.10, s32[1,96]{1,0:T(1,128)} %bitcast.13, bf16[384,1408]{1,0:T(8,128)(2,1)} %hid_ref.1, f32[1,1408]{1,0:T(1,128)} %broadcast_in_dim.46.ob_ref, ...), custom_call_target="tpu_custom_call" | custom-call | tf_op jit(solution)/shard_map/layer/pallas_call | solution.py:392
  108.7 0.0 copy-done
  108.7 0.1 broadcast_compare_fusion
  108.8 0.8 select_reduce_fusion
  109.6 0.6 slice.11
  110.2 0.7 slice_reduce_fusion
  110.9 1.6 %copy.20 = bf16[96,1024]{1,0:T(8,128)(2,1)} copy(bf16[96,1024]{1,0:T(8,128)(2,1)} %get-tuple-element.10) | data formatting | bytes 393216
  (1 shorter events, 0.0 us)
Async XLA Ops:
  7.1 101.6 %copy-start = (s32[16]{0:T(128)S(1)}, s32[16]{0:T(128)}, u32[]{:S(2)}) copy-start(s32[16]{0:T(128)} %param.31) | copy-start | bytes 196

commit v3 on v2

--- a/solution.py
+++ b/solution.py
@@ -90,8 +90,7 @@
         pltpu.make_async_copy(src, dst, load_sem.at[i])
         for i, (src, dst) in enumerate(((ow_hbm, ow), (up_hbm, up), (dn_hbm, dn), (mg_hbm, mg)))
     ]
-    for load in loads:
-        load.start()
+    loads[0].start()
 
     barrier = pltpu.get_barrier_semaphore()
     for k in (1, 2, 3):
@@ -180,13 +179,42 @@
         lax.fori_loop(1, parts, one, 0)
 
     pass_all(0)
+    core = lax.rem(blk, 2)
+    half = 2 * ROWS
+
+    def weight_out(k):
+        rows = pl.ds(pl.multiple_of(core * half, half), half)
+        return pltpu.make_async_remote_copy(
+            src_ref=owp.at[hg, rows],
+            dst_ref=owp.at[hg, rows],
+            send_sem=send_sem.at[6, k],
+            recv_sem=recv_sem.at[6, k],
+            device_id={"head": head_peer(hg, k)},
+            device_id_type=MESH,
+        )
+
+    def weight_on(k):
+        rows = pl.ds(pl.multiple_of(core * half, half), half)
+        return pltpu.make_async_remote_copy(
+            src_ref=owp.at[head_peer(hg, k), rows],
+            dst_ref=owp.at[head_peer(hg, k), rows],
+            send_sem=send_sem.at[7, k],
+            recv_sem=recv_sem.at[7, k],
+            device_id={"blk": blk + 1 - 2 * core},
+            device_id_type=MESH,
+        )
+
     loads[0].wait()
     whole = ow[...].astype(F32)
     for h in range(4):
         padded = jnp.concatenate(
             [whole[h * HD : (h + 1) * HD], jnp.zeros((ROWS - HD, width), F32)], axis=0
         )
-        owp[h * ROWS : (h + 1) * ROWS] = padded.astype(BF16)
+        owp[hg, h * ROWS : (h + 1) * ROWS] = padded.astype(BF16)
+    for k in (3, 1, 2):
+        weight_out(k).start()
+    for load in loads[1:]:
+        load.start()
     for i in (1, 3, 2):
         scatter(i).wait_recv()
         pass_all(i)
@@ -238,6 +266,10 @@
             top = jnp.maximum(top, jnp.max(inside, axis=1, keepdims=True))
         if i > 0:
             give_back(i).start()
+        if i == 1:
+            for k in (1, 2, 3):
+                weight_out(k).wait_recv()
+                weight_on(k).start()
     att[pl.ds(pl.multiple_of(mine * ROWS, ROWS), ROWS)] = asend[mine]
 
     row = lax.broadcasted_iota(jnp.int32, (groups, tokens), 0)
@@ -246,27 +278,26 @@
     def pick(k):
         return jnp.where(col == 4 * row + head_peer(hg, k), 1.0, 0.0).astype(BF16)
 
-    total = nn_dot(pick(0), hid_ref[...]) + ob_ref[...]
+    total = nn_dot(pick(0), hid_ref[...]) + ob_ref[...].reshape(1, -1)
     for i in (1, 2, 3):
         give_back(i).wait_recv()
-    for k in (3, 1, 2, 0):
-        rows = nt_dot(pick(k), att[...]).astype(BF16)
-        term = nn_dot(rows, owp[...])
-        if k == 0:
-            total = total + term
-        else:
-            psend[k] = term.astype(BF16)
-            exchange(0, psend.at[k], precv, k).start()
+    for k in (3, 1, 2):
+        psend[k] = nt_dot(pick(k), att[...]).astype(BF16)
+        exchange(0, psend.at[k], precv, k).start()
+    own_rows = nt_dot(pick(0), att[...]).astype(BF16)
+    total = total + nn_dot(own_rows, owp[hg])
+    for k in (1, 2, 3):
+        weight_on(k).wait_recv()
     for k in (1, 2, 3):
         exchange(0, psend.at[k], precv, k).wait_recv()
-        total = total + precv[k].astype(F32)
+        total = total + nn_dot(precv[k], owp[head_peer(hg, k)])
     mean = jnp.mean(total, axis=-1, keepdims=True)
     centered = total - mean
     var = jnp.mean(centered * centered, axis=-1, keepdims=True)
-    nbuf[0] = (centered * lax.rsqrt(var + EPSILON) * gain_ref[...] + nb_ref[...]).astype(BF16)
+    nbuf[0] = (centered * lax.rsqrt(var + EPSILON) * gain_ref[...].reshape(1, -1) + nb_ref[...].reshape(1, -1)).astype(BF16)
     for k in (3, 1, 2):
         exchange(1, nbuf.at[0], nbuf, k).start()
-    mixed[...] = total + db_ref[...]
+    mixed[...] = total + db_ref[...].reshape(1, -1)
 
     loads[1].wait()
     loads[2].wait()
@@ -276,7 +307,7 @@
         def _():
             exchange(1, nbuf.at[0], nbuf, k).wait_recv()
 
-        units = nn_dot(nbuf[k], up[...]) + ub_ref[...]
+        units = nn_dot(nbuf[k], up[...]) + ub_ref[...].reshape(1, -1)
         units = (0.5 * units * (1.0 + lax.erf(units * math.sqrt(0.5)))).astype(BF16)
         term = nn_dot(units, dn[...])
 
@@ -302,7 +333,7 @@
         exchange(3, sbuf.at[0], sbuf, k).start()
     squares[...] = jnp.sum(state * state, axis=-1, keepdims=True)
     loads[3].wait()
-    merged[...] = mb_ref[...] + nn_dot(sbuf[0], mg[hg])
+    merged[...] = mb_ref[...].reshape(1, -1) + nn_dot(sbuf[0], mg[hg])
 
     for k in (1, 2, 3):
         exchange(3, sbuf.at[0], sbuf, k).wait_recv()
@@ -361,6 +392,8 @@
     for k in (1, 2, 3):
         scatter(k).wait_send()
         give_back(k).wait_send()
+        weight_out(k).wait_send()
+        weight_on(k).wait_send()
         exchange(0, psend.at[k], precv, k).wait_send()
         exchange(1, nbuf.at[0], nbuf, k).wait_send()
         exchange(2, dsend.at[k], drecv, k).wait_send()
@@ -402,14 +435,14 @@
             pltpu.VMEM(up.shape, BF16),
             pltpu.VMEM(dn.shape, BF16),
             pltpu.VMEM(mg.shape, BF16),
-            pltpu.VMEM((4 * ROWS, width), BF16),
+            pltpu.VMEM((4, 4 * ROWS, width), BF16),
             pltpu.VMEM((4, 3, ROWS, tokens), BF16),
             pltpu.VMEM((n, 3, ROWS, tokens), BF16),
             pltpu.VMEM((n, tokens, tile), F32),
             pltpu.VMEM((4, ROWS, tokens), BF16),
             pltpu.VMEM((4 * ROWS, tokens), BF16),
-            chunk,
-            chunk,
+            pltpu.VMEM((4, groups, 4 * ROWS), BF16),
+            pltpu.VMEM((4, groups, 4 * ROWS), BF16),
             chunk,
             chunk,
             chunk,
@@ -419,8 +452,8 @@
             pltpu.VMEM((groups, 1), F32),
             pltpu.VMEM((n, requests, 128), F32),
             pltpu.SemaphoreType.DMA((4,)),
-            pltpu.SemaphoreType.DMA((6, 4)),
-            pltpu.SemaphoreType.DMA((6, 4)),
+            pltpu.SemaphoreType.DMA((8, 4)),
+            pltpu.SemaphoreType.DMA((8, 4)),
             pltpu.SemaphoreType.DMA((n,)),
             pltpu.SemaphoreType.DMA((n,)),
             pltpu.SemaphoreType.DMA((4, parts)),
@@ -462,12 +495,12 @@
             values.T,
             group_segments[None],
             hidden_in,
-            out_bias[None],
-            norm_gain[None],
-            norm_bias[None],
-            up_bias[None],
-            down_bias[None],
-            merge_bias[None],
+            out_bias,
+            norm_gain,
+            norm_bias,
+            up_bias,
+            down_bias,
+            merge_bias,
         ),
         (out_weight, up_weight, down_weight, merge_weight.reshape(4, model_width, -1)),
         blk_count,

time: 114 us -> 97.9 us (0.86); the launches traced: 113 us -> 97.7 us
  Pallas kernels: 102 us -> 93.2 us
  local copies, waits for them, and re-layouts: 9.41 us -> 2.95 us
    pallas_call x1, Pallas kernels: 102 us -> 93.2 us  [layer(): pl.pallas_call(functools.partial(layer_kernel, n, parts, requests), out_s...]
    broadcast_in_dim x5 -> x0, local copies, waits for them, and re-layouts: 6.46 us -> none  [the longest x1 1.3 us: body(): norm_gain[None]]
where the time goes in v3:
time: 97.9 us; the launch traced here: 97.7 us
  Pallas kernels  93.2 us (95%)
  local copies, waits for them, and re-layouts  2.95 us (3%)
    pallas_call x1, Pallas kernels, layer(): pl.pallas_call(functools.partial(layer_kernel, n, parts, requests), out_s...  93.2 us

profile of v3, /device:TPU:0, one launch (start us, length us, event | category | flops | bytes accessed | tf_op | source)
XLA Modules:
  0.0 97.7 jit_solution(6503558115554139498)
XLA Ops:
  0.6 0.0 copy-start
  0.6 93.2 %layer.1 = (bf16[96,1024]{1,0:T(8,128)(2,1)}, f32[16,128]{1,0:T(8,128)}) custom-call(bf16[352,384]{1,0:T(8,128)(2,1)} %bitcast.7, bf16[352,384]{1,0:T(8,128)(2,1)} %bitcast.8, bf16[352,384]{1,0:T(8,128)(2,1)} %bitcast.9, s32[1,96]{1,0:T(1,128)} %bitcast.11, bf16[384,1408]{1,0:T(8,128)(2,1)} %hid_ref.1, f32[1408]{0:T(1024)} %ob_ref.1, f32[1408]{0:T(1024)} %gain_ref.1, ...), custom_call_target="tpu_custom_call" | custom-call | tf_op jit(solution)/shard_map/layer/pallas_call | solution.py:425
  93.9 0.0 copy-done
  93.9 0.1 broadcast_compare_fusion
  93.9 0.8 select_reduce_fusion
  94.7 0.6 slice.11
  95.4 0.7 slice_reduce_fusion
  96.1 1.6 %copy.20 = bf16[96,1024]{1,0:T(8,128)(2,1)} copy(bf16[96,1024]{1,0:T(8,128)(2,1)} %get-tuple-element.10) | data formatting | bytes 393216
  (1 shorter events, 0.0 us)
Async XLA Ops:
  0.6 93.2 %copy-start = (s32[16]{0:T(128)S(1)}, s32[16]{0:T(128)}, u32[]{:S(2)}) copy-start(s32[16]{0:T(128)} %param.31) | copy-start | bytes 196

commit v4 on v3

--- a/solution.py
+++ b/solution.py
@@ -60,6 +60,8 @@
     xsend,
     x,
     scores,
+    acc,
+    peak,
     asend,
     att,
     psend,
@@ -215,61 +217,89 @@
         weight_out(k).start()
     for load in loads[1:]:
         load.start()
-    for i in (1, 3, 2):
-        scatter(i).wait_recv()
-        pass_all(i)
-    for i in range(4):
-
-        def landed(j, carry):
-            hand_on(i, j).wait_recv()
-            return carry
-
-        lax.fori_loop(1, parts, landed, 0)
-
     rate = HD ** (-0.5)
     speed = rate * math.log2(math.e)
     shift = bits * CODE * CODE
     tile = scores.shape[2]
-    names = lax.broadcasted_iota(jnp.int32, (requests, tile), 0).astype(F32)
+    names = lax.broadcasted_iota(jnp.int32, (requests, tokens), 0).astype(F32)
     weights_of = jnp.where(
-        lax.broadcasted_iota(jnp.int32, (8, tile), 0) < bits,
-        lax.shift_left(1, lax.broadcasted_iota(jnp.int32, (8, tile), 0)).astype(F32),
+        code_row < bits,
+        lax.shift_left(1, code_row).astype(F32),
         0.0,
     )
     top = jnp.full((requests, 1), NEGATIVE, F32)
-    for i in (2, 1, 3, 0):
-        goal = lax.rem(mine + i, 4)
+    def owner(i):
+        return lax.rem(mine + 4 - i, 4)
+
+    def landed(i):
+        def one(j, carry):
+            hand_on(i, j).wait_recv()
+            return carry
+
+        lax.fori_loop(1, parts, one, 0)
+
+    def update(qi, sets, fresh):
         for at in range(0, tokens, tile):
-            query = x[goal * parts + part, 2, :, at : at + tile]
-
-            def score(b, best):
-                got = lax.dot_general(
-                    x[b, 0], query, (((0,), (0,)), ((), ())), preferred_element_type=F32
-                )
-                scores[b] = got
-                return jnp.maximum(best, jnp.max(got, axis=0, keepdims=True))
-
-            best = lax.fori_loop(
-                0, blk_count, score, jnp.full((1, tile), NEGATIVE, F32), unroll=4
-            )
+            span = slice(at, at + tile)
+            query = x[owner(qi) * parts + part, 2, :, span]
+            best = jnp.full((1, tile), NEGATIVE, F32) if fresh else peak[qi, :, span]
+            before = best
+            for place, si in enumerate(sets):
+
+                def score(j, best):
+                    keys = x[owner(si) * parts + j, 0]
+                    got = lax.dot_general(
+                        keys, query, (((0,), (0,)), ((), ())), preferred_element_type=F32
+                    )
+                    scores[place * parts + j] = got
+                    return jnp.maximum(best, jnp.max(got, axis=0, keepdims=True))
+
+                best = lax.fori_loop(0, parts, score, best, unroll=2)
             base = best * speed
-
-            def blend(b, total):
-                weight = jnp.exp2(scores[b] * speed - base).astype(BF16)
-                return total + nn_dot(x[b, 1], weight)
-
-            total = lax.fori_loop(0, blk_count, blend, jnp.zeros((ROWS, tile), F32), unroll=4)
-            asend[goal, :, at : at + tile] = (total / total[HD : HD + 1]).astype(BF16)
-            marks = query.astype(F32)[HD:ROWS]
-            name = jnp.sum(jnp.where(marks > 0, weights_of, 0.0), axis=0, keepdims=True)
-            inside = jnp.where(names == name, (best - shift) * rate, NEGATIVE)
-            top = jnp.maximum(top, jnp.max(inside, axis=1, keepdims=True))
-        if i > 0:
-            give_back(i).start()
-        if i == 1:
-            for k in (1, 2, 3):
-                weight_out(k).wait_recv()
-                weight_on(k).start()
+            if fresh:
+                total = jnp.zeros((ROWS, tile), F32)
+            else:
+                total = acc[qi, :, span] * jnp.exp2(before * speed - base)
+            for place, si in enumerate(sets):
+
+                def blend(j, total):
+                    weight = jnp.exp2(scores[place * parts + j] * speed - base).astype(BF16)
+                    return total + nn_dot(x[owner(si) * parts + j, 1], weight)
+
+                total = lax.fori_loop(0, parts, blend, total, unroll=2)
+            acc[qi, :, span] = total
+            peak[qi, :, span] = best
+
+    def finish(qi, top):
+        goal = owner(qi)
+        total = acc[qi]
+        asend[goal] = (total / total[HD : HD + 1]).astype(BF16)
+        if qi > 0:
+            give_back(4 - qi).start()
+        marks = x[goal * parts + part, 2].astype(F32)[HD:ROWS]
+        name = jnp.sum(jnp.where(marks > 0, weights_of, 0.0), axis=0, keepdims=True)
+        inside = jnp.where(names == name, (peak[qi] - shift) * rate, NEGATIVE)
+        return jnp.maximum(top, jnp.max(inside, axis=1, keepdims=True))
+
+    landed(0)
+    update(0, (0,), True)
+    for at, i in ((1, 1), (2, 3), (3, 2)):
+        seen = (0, 1, 3)[:at]
+        scatter(i).wait_recv()
+        pass_all(i)
+        update(i, seen, True)
+        landed(i)
+        update(i, (i,), False)
+        if at < 3:
+            for qi in seen:
+                update(qi, (i,), False)
+    top = finish(2, top)
+    for k in (1, 2, 3):
+        weight_out(k).wait_recv()
+        weight_on(k).start()
+    for qi in (1, 3, 0):
+        update(qi, (2,), False)
+        top = finish(qi, top)
     att[pl.ds(pl.multiple_of(mine * ROWS, ROWS), ROWS)] = asend[mine]
 
     row = lax.broadcasted_iota(jnp.int32, (groups, tokens), 0)
@@ -295,7 +325,7 @@
     centered = total - mean
     var = jnp.mean(centered * centered, axis=-1, keepdims=True)
     nbuf[0] = (centered * lax.rsqrt(var + EPSILON) * gain_ref[...].reshape(1, -1) + nb_ref[...].reshape(1, -1)).astype(BF16)
-    for k in (3, 1, 2):
+    for k in (1, 2, 3):
         exchange(1, nbuf.at[0], nbuf, k).start()
     mixed[...] = total + db_ref[...].reshape(1, -1)
 
@@ -329,7 +359,7 @@
         exchange(2, dsend.at[k], drecv, k).wait_recv()
         state = state + drecv[k].astype(F32)
     sbuf[0] = state.astype(BF16)
-    for k in (3, 1, 2):
+    for k in (1, 2, 3):
         exchange(3, sbuf.at[0], sbuf, k).start()
     squares[...] = jnp.sum(state * state, axis=-1, keepdims=True)
     loads[3].wait()
@@ -339,6 +369,8 @@
         exchange(3, sbuf.at[0], sbuf, k).wait_recv()
         piece = sbuf[k].astype(F32)
         squares[...] += jnp.sum(piece * piece, axis=-1, keepdims=True)
+        if k < 3:
+            merged[...] += nn_dot(sbuf[k], mg[head_peer(hg, k)])
     ids = lax.broadcasted_iota(jnp.int32, (requests, groups), 0)
     member = jnp.where(seg_ref[...] == ids, 1.0, 0.0)
     sums = jnp.dot(
@@ -367,12 +399,7 @@
 
     lax.fori_loop(1, blk_count, stat_start, 0)
 
-    def merge(k, carry):
-        merged[...] += nn_dot(sbuf[k], mg[head_peer(hg, k)])
-        return carry
-
-    lax.fori_loop(1, 4, merge, 0)
-    out_ref[...] = merged[...].astype(BF16)
+    out_ref[...] = (merged[...] + nn_dot(sbuf[3], mg[head_peer(hg, 3)])).astype(BF16)
 
     def fold(i, carry):
         added, best = carry
@@ -439,6 +466,8 @@
             pltpu.VMEM((4, 3, ROWS, tokens), BF16),
             pltpu.VMEM((n, 3, ROWS, tokens), BF16),
             pltpu.VMEM((n, tokens, tile), F32),
+            pltpu.VMEM((4, ROWS, tokens), F32),
+            pltpu.VMEM((4, 1, tokens), F32),
             pltpu.VMEM((4, ROWS, tokens), BF16),
             pltpu.VMEM((4 * ROWS, tokens), BF16),
             pltpu.VMEM((4, groups, 4 * ROWS), BF16),

time: 97.9 us -> 97.6 us (level)
  no operation moved by 1% of the time
where the time goes in v4:
time: 97.6 us; the launch traced here: 97.4 us
  Pallas kernels  92.9 us (95%)
  local copies, waits for them, and re-layouts  2.95 us (3%)
    pallas_call x1, Pallas kernels, layer(): pl.pallas_call(functools.partial(layer_kernel, n, parts, requests), out_s...  92.9 us

profile of v4, /device:TPU:0, one launch (start us, length us, event | category | flops | bytes accessed | tf_op | source)
XLA Modules:
  0.0 97.4 jit_solution(10002631216778234544)
XLA Ops:
  0.6 0.0 copy-start
  0.6 92.9 %layer.1 = (bf16[96,1024]{1,0:T(8,128)(2,1)}, f32[16,128]{1,0:T(8,128)}) custom-call(bf16[352,384]{1,0:T(8,128)(2,1)} %bitcast.7, bf16[352,384]{1,0:T(8,128)(2,1)} %bitcast.8, bf16[352,384]{1,0:T(8,128)(2,1)} %bitcast.9, s32[1,96]{1,0:T(1,128)} %bitcast.11, bf16[384,1408]{1,0:T(8,128)(2,1)} %hid_ref.1, f32[1408]{0:T(1024)} %ob_ref.1, f32[1408]{0:T(1024)} %gain_ref.1, ...), custom_call_target="tpu_custom_call" | custom-call | tf_op jit(solution)/shard_map/layer/pallas_call | solution.py:452
  93.6 0.0 copy-done
  93.6 0.1 broadcast_compare_fusion
  93.7 0.8 select_reduce_fusion
  94.5 0.6 slice.11
  95.1 0.7 slice_reduce_fusion
  95.8 1.6 %copy.20 = bf16[96,1024]{1,0:T(8,128)(2,1)} copy(bf16[96,1024]{1,0:T(8,128)(2,1)} %get-tuple-element.10) | data formatting | bytes 393216
  (1 shorter events, 0.0 us)
Async XLA Ops:
  0.6 93.0 %copy-start = (s32[16]{0:T(128)S(1)}, s32[16]{0:T(128)}, u32[]{:S(2)}) copy-start(s32[16]{0:T(128)} %param.31) | copy-start | bytes 196

commit v5 on v4

--- a/solution.py
+++ b/solution.py
@@ -72,7 +72,7 @@
     sbuf,
     mixed,
     merged,
-    squares,
+    hstat,
     gstat,
     load_sem,
     send_sem,
@@ -359,27 +359,15 @@
         exchange(2, dsend.at[k], drecv, k).wait_recv()
         state = state + drecv[k].astype(F32)
     sbuf[0] = state.astype(BF16)
-    for k in (1, 2, 3):
-        exchange(3, sbuf.at[0], sbuf, k).start()
-    squares[...] = jnp.sum(state * state, axis=-1, keepdims=True)
-    loads[3].wait()
-    merged[...] = mb_ref[...].reshape(1, -1) + nn_dot(sbuf[0], mg[hg])
-
-    for k in (1, 2, 3):
-        exchange(3, sbuf.at[0], sbuf, k).wait_recv()
-        piece = sbuf[k].astype(F32)
-        squares[...] += jnp.sum(piece * piece, axis=-1, keepdims=True)
-        if k < 3:
-            merged[...] += nn_dot(sbuf[k], mg[head_peer(hg, k)])
     ids = lax.broadcasted_iota(jnp.int32, (requests, groups), 0)
     member = jnp.where(seg_ref[...] == ids, 1.0, 0.0)
     sums = jnp.dot(
         member,
-        jnp.broadcast_to(squares[...], (groups, 128)),
+        jnp.broadcast_to(jnp.sum(state * state, axis=-1, keepdims=True), (groups, 128)),
         preferred_element_type=F32,
         precision=lax.Precision.HIGHEST,
     )
-    counts = 4.0 * jnp.sum(member, axis=1, keepdims=True)
+    counts = jnp.sum(member, axis=1, keepdims=True)
     lane = lax.broadcasted_iota(jnp.int32, (requests, 128), 1)
     gstat[0] = jnp.where(lane == 0, top, jnp.where(lane == 1, sums, counts))
 
@@ -399,7 +387,10 @@
 
     lax.fori_loop(1, blk_count, stat_start, 0)
 
-    out_ref[...] = (merged[...] + nn_dot(sbuf[3], mg[head_peer(hg, 3)])).astype(BF16)
+    for k in (1, 2, 3):
+        exchange(3, sbuf.at[0], sbuf, k).start()
+    loads[3].wait()
+    merged[...] = mb_ref[...].reshape(1, -1) + nn_dot(sbuf[0], mg[hg])
 
     def fold(i, carry):
         added, best = carry
@@ -413,6 +404,19 @@
 
     start = (jnp.zeros((requests, 128), F32), jnp.full((requests, 128), NEGATIVE, F32))
     added, best = lax.fori_loop(1, blk_count, stat_wait, fold(0, start))
+    hstat[0] = added
+    for k in (1, 2, 3):
+        exchange(8, hstat.at[0], hstat, k).start()
+
+    for k in (1, 2, 3):
+        exchange(3, sbuf.at[0], sbuf, k).wait_recv()
+        if k < 3:
+            merged[...] += nn_dot(sbuf[k], mg[head_peer(hg, k)])
+    out_ref[...] = (merged[...] + nn_dot(sbuf[3], mg[head_peer(hg, 3)])).astype(BF16)
+
+    for k in (1, 2, 3):
+        exchange(8, hstat.at[0], hstat, k).wait_recv()
+        added = added + hstat[k]
     rms = jnp.sqrt(added[:, 1:2] / (jnp.maximum(added[:, 2:3], 1.0) * width) + EPSILON)
     stat_ref[...] = jnp.where(lane == 1, rms, best)
 
@@ -425,6 +429,7 @@
         exchange(1, nbuf.at[0], nbuf, k).wait_send()
         exchange(2, dsend.at[k], drecv, k).wait_send()
         exchange(3, sbuf.at[0], sbuf, k).wait_send()
+        exchange(8, hstat.at[0], hstat, k).wait_send()
     for i in range(4):
 
         def passed(j, carry):
@@ -478,11 +483,11 @@
             chunk,
             pltpu.VMEM((groups, width), F32),
             pltpu.VMEM((groups, mg.shape[2]), F32),
-            pltpu.VMEM((groups, 1), F32),
+            pltpu.VMEM((4, requests, 128), F32),
             pltpu.VMEM((n, requests, 128), F32),
             pltpu.SemaphoreType.DMA((4,)),
-            pltpu.SemaphoreType.DMA((8, 4)),
-            pltpu.SemaphoreType.DMA((8, 4)),
+            pltpu.SemaphoreType.DMA((9, 4)),
+            pltpu.SemaphoreType.DMA((9, 4)),
             pltpu.SemaphoreType.DMA((n,)),
             pltpu.SemaphoreType.DMA((n,)),
             pltpu.SemaphoreType.DMA((4, parts)),

time: 97.6 us -> 92.4 us (0.947)
  Pallas kernels: 92.9 us -> 87.7 us
    pallas_call x1, Pallas kernels: 92.9 us -> 87.7 us  [layer(): pl.pallas_call(functools.partial(layer_kernel, n, parts, requests), out_s...]
where the time goes in v5:
time: 92.4 us; the launch traced here: 92.2 us
  Pallas kernels  87.7 us (95%)
  local copies, waits for them, and re-layouts  2.95 us (3%)
    pallas_call x1, Pallas kernels, layer(): pl.pallas_call(functools.partial(layer_kernel, n, parts, requests), out_s...  87.7 us

profile of v5, /device:TPU:0, one launch (start us, length us, event | category | flops | bytes accessed | tf_op | source)
XLA Modules:
  0.0 92.2 jit_solution(4659131824617358585)
XLA Ops:
  0.6 0.0 copy-start
  0.6 87.7 %layer.1 = (bf16[96,1024]{1,0:T(8,128)(2,1)}, f32[16,128]{1,0:T(8,128)}) custom-call(bf16[352,384]{1,0:T(8,128)(2,1)} %bitcast.7, bf16[352,384]{1,0:T(8,128)(2,1)} %bitcast.8, bf16[352,384]{1,0:T(8,128)(2,1)} %bitcast.9, s32[1,96]{1,0:T(1,128)} %bitcast.11, bf16[384,1408]{1,0:T(8,128)(2,1)} %hid_ref.1, f32[1408]{0:T(1024)} %ob_ref.1, f32[1408]{0:T(1024)} %gain_ref.1, ...), custom_call_target="tpu_custom_call" | custom-call | tf_op jit(solution)/shard_map/layer/pallas_call | solution.py:457
  88.4 0.0 copy-done
  88.4 0.1 broadcast_compare_fusion
  88.5 0.8 select_reduce_fusion
  89.3 0.6 slice.11
  89.9 0.7 slice_reduce_fusion
  90.6 1.6 %copy.20 = bf16[96,1024]{1,0:T(8,128)(2,1)} copy(bf16[96,1024]{1,0:T(8,128)(2,1)} %get-tuple-element.10) | data formatting | bytes 393216
  (1 shorter events, 0.0 us)
Async XLA Ops:
  0.6 87.8 %copy-start = (s32[16]{0:T(128)S(1)}, s32[16]{0:T(128)}, u32[]{:S(2)}) copy-start(s32[16]{0:T(128)} %param.31) | copy-start | bytes 196
